TPU v7x, 32 devices: a whole 2x2x4 slice. The times are simulated.
32 devices in a mesh: ens: 2 (over x), lat: 4 (over y, core), lon: 4 (over z).
Axes of the slice: x: 2, y: 2, z: 4, core: 2. Of those that a mesh axis runs over, the one named last changes fastest.
Arguments:
- members_in: bfloat16 [8, 32, 64, 256], P('ens', 'lat', 'lon'), may hold values from -6 to 6
- out_grad: bfloat16 [8, 32, 64, 256], P('ens', 'lat', 'lon'), may hold values from -6 to 6
- weight: bfloat16 [9, 256, 256], replicated, may hold values from -0.125 to 0.125
- basis_blocks: float32 [8, 9, 3, 9], replicated, may hold values from -1.75 to 1.75
- cycle_block: int32 [32], replicated, may hold values from 0 to 7
- half_width: int32 [32, 3], replicated, may hold values from 1 to 4
Outputs:
- result: bfloat16 [8, 32, 64, 256], P('ens', 'lat', 'lon')
- in_grad: bfloat16 [8, 32, 64, 256], P('ens', 'lat', 'lon')
- weight_grad: float32 [9, 256, 256], P(None, 'lon')
All inputs are finite; a program needn't handle non-finite values.
Results may differ from a plain program's by a relative error of at most 0.015.
Values may be sent and summed in bfloat16 or wider, within the bound.
A program may use at most 64 MiB of HBM per device.

v0:
```python
import math

import jax
import jax.numpy as jnp
from jax import lax
from jax.sharding import PartitionSpec as P

C = 256
K = 9
R = 1
H = 4


def extended(block, sides, width, periodic):
    for axis, dim in sides:
        count = lax.axis_size(axis)
        forward = [(i, i + 1) for i in range(count - 1)]
        if periodic:
            forward.append((count - 1, 0))
        backward = [(target, source) for source, target in forward]
        low = lax.ppermute(
            lax.slice_in_dim(block, block.shape[dim] - width, None, axis=dim), axis, forward
        )
        high = lax.ppermute(lax.slice_in_dim(block, 0, width, axis=dim), axis, backward)
        block = jnp.concatenate([low, block, high], axis=dim)
    return block


def local_table(basis_blocks, cycle_block, half_width, first_cycle, cycle_count):
    total_cycles = cycle_block.shape[0]
    cycle_ids = jnp.clip(
        first_cycle + jnp.arange(cycle_count, dtype=jnp.int32), 0, total_cycles - 1
    )
    one_hot = (cycle_ids[:, None] == jnp.arange(total_cycles, dtype=jnp.int32)[None, :]).astype(
        jnp.int32
    )
    block_ids = jnp.sum(one_hot * cycle_block[None, :], axis=1)
    widths = jnp.sum(one_hot[:, :, None] * half_width[None, :, :], axis=1)
    block_count = basis_blocks.shape[0]
    pick_block = (block_ids[:, None] == jnp.arange(block_count, dtype=jnp.int32)[None, :]).astype(
        jnp.float32
    )
    picked = jnp.dot(
        pick_block,
        basis_blocks.reshape(block_count, -1),
        precision=lax.Precision.HIGHEST,
        preferred_element_type=jnp.float32,
    )
    picked = picked.reshape((cycle_count,) + basis_blocks.shape[1:])
    offsets = jnp.arange(2 * H + 1, dtype=jnp.int32) - H
    inside = jnp.abs(offsets)[None, None, :] <= widths[:, :, None]
    return (jnp.where(inside[:, None, :, :], picked, jnp.float32(0.0)), widths)


def extend(values):
    tall_block = extended(values, (("lat", 1),), R, False)
    return extended(tall_block, (("lon", 2),), H, True)


def spread_forward(padded, coefficients, half_reach):
    lat_rows = padded.shape[1] - 2 * R
    lon_cols = padded.shape[2] - 2 * H

    def single(member):
        summed = jnp.zeros(
            (lat_rows, lon_cols, coefficients.shape[1], member.shape[-1]), jnp.float32
        )
        for offset_row in range(2 * R + 1):
            for offset_col in range(H - half_reach, H + half_reach + 1):
                sliced = member[
                    offset_row : offset_row + lat_rows, offset_col : offset_col + lon_cols
                ]
                summed = summed + coefficients[:, None, :, offset_row, offset_col, None] * sliced[
                    :, :, None, :
                ].astype(jnp.float32)
        return summed.astype(jnp.bfloat16)

    return lax.map(single, padded)


def spread_adjoint(padded, coefficients, half_reach):
    lat_rows = padded.shape[1] - 2 * R
    lon_cols = padded.shape[2] - 2 * H

    def single(member):
        summed = jnp.zeros(
            (lat_rows, lon_cols, coefficients.shape[1], member.shape[-1]), jnp.float32
        )
        for offset_row in range(2 * R + 1):
            lead_row = 2 * R - offset_row
            rows_coef = coefficients[lead_row : lead_row + lat_rows]
            for offset_col in range(H - half_reach, H + half_reach + 1):
                lead_col = 2 * H - offset_col
                sliced = member[lead_row : lead_row + lat_rows, lead_col : lead_col + lon_cols]
                summed = summed + rows_coef[:, None, :, offset_row, offset_col, None] * sliced[
                    :, :, None, :
                ].astype(jnp.float32)
        return summed.astype(jnp.bfloat16)

    return lax.map(single, padded)


def apply_spread(kernel, padded, coefficients):
    return kernel(padded, coefficients, H)


def shards(members_in, out_grad, weight, basis_blocks, cycle_block, half_width):
    members, lat_rows, lon_cols, channels = members_in.shape
    first_cycle = lax.axis_index("lat") * lat_rows
    wide_coef, wide_widths = local_table(
        basis_blocks, cycle_block, half_width, first_cycle - R, lat_rows + 2 * R
    )
    own_coef = wide_coef[R : R + lat_rows]
    padded_in = extend(members_in)
    features = apply_spread(spread_forward, padded_in, own_coef)
    feature_rows = features.reshape(members * lat_rows * lon_cols, K * C)
    mixed = jnp.dot(feature_rows, weight.reshape(K * C, C), preferred_element_type=jnp.float32)
    activated, slope_fn = jax.vjp(jax.nn.gelu, mixed)
    cot_rows = out_grad.reshape(-1, channels).astype(jnp.float32)
    result = (members_in.reshape(-1, channels).astype(jnp.float32) + activated).astype(jnp.bfloat16)
    grad_mixed = slope_fn(cot_rows)[0].astype(jnp.bfloat16)
    cell_count = (
        members
        * lax.axis_size("ens")
        * lat_rows
        * lax.axis_size("lat")
        * lon_cols
        * lax.axis_size("lon")
    )
    local_grad = lax.dot_general(
        feature_rows, grad_mixed, (((0,), (0,)), ((), ())), preferred_element_type=jnp.float32
    )
    local_grad = (local_grad * (1.0 / math.sqrt(cell_count))).reshape(K, C, C)
    share_grad = lax.psum_scatter(
        local_grad.astype(jnp.bfloat16), "lon", scatter_dimension=1, tiled=True
    )
    weight_grad = lax.psum(share_grad, ("ens", "lat")).astype(jnp.float32)
    padded_grad = extend(grad_mixed.reshape(members, lat_rows, lon_cols, channels))
    back = apply_spread(spread_adjoint, padded_grad, wide_coef)
    branch_rows = lax.dot_general(
        back.reshape(-1, K, C),
        weight,
        (((1, 2), (0, 2)), ((), ())),
        preferred_element_type=jnp.float32,
    )
    in_grad = (cot_rows + branch_rows).astype(jnp.bfloat16)
    return (result.reshape(members_in.shape), in_grad.reshape(members_in.shape), weight_grad)


def solution(mesh):
    return jax.shard_map(
        shards,
        mesh=mesh,
        in_specs=(P("ens", "lat", "lon", None), P("ens", "lat", "lon", None), P(), P(), P(), P()),
        out_specs=(
            P("ens", "lat", "lon", None),
            P("ens", "lat", "lon", None),
            P(None, "lon", None),
        ),
        check_vma=False,
    )
```

profile of v0, /device:TPU:0, one launch (start us, length us, event | category | flops | bytes accessed | tf_op | source)
XLA Modules:
  0.0 165.7 jit_solution(14828743148035641486)
XLA Ops:
  7.2 0.9 fusion.32
  8.1 1.3 collective-permute-start.1
  9.4 3.0 %collective-permute-start = (bf16[4,1,16,256]{3,2,1,0:T(8,128)(2,1)S(1)}, bf16[4,1,16,256]{3,2,1,0:T(8,128)(2,1)S(1)}, u32[]{:S(2)}, u32[]{:S(2)}) collective-permute-start(bf16[4,1,16,256]{3,2,1,0:T(8,128)(2,1)S(1)} %get-tuple-element.206), channel_id=1, source_target_pairs={{0,4},{4,8},{8,12},{1,5},{5,9},{9,13},{2,6},{6,10},{10,14},{3,7},{... | collective-permute-start | bytes 98312 | tf_op jit(solution)/shard_map/ppermute | solution.py:21
  12.5 0.1 fusion.26
  12.5 0.9 multiply_reduce_fusion
  13.5 0.1 copy.19
  13.5 0.1 broadcast_compare_fusion
  13.6 0.8 select_reduce_fusion
  14.5 0.9 copy.20
  15.4 0.1 reshape.559
  15.5 0.1 dot_general.17
  15.7 1.0 constant_dynamic-update-slice_fusion.1
  16.7 0.1 fusion.30
  16.8 3.1 %collective-permute-start.2 = (bf16[4,10,4,256]{3,2,1,0:T(4,128)(2,1)S(1)}, bf16[4,10,4,256]{3,2,1,0:T(4,128)(2,1)S(1)}, u32[]{:S(2)}, u32[]{:S(2)}) collective-permute-start(bf16[4,10,4,256]{3,2,1,0:T(4,128)(2,1)S(1)} %get-tuple-element.201), channel_id=1, source_target_pairs={{0,1},{1,2},{2,3},{3,0},{4,5},{5,6},{6,7},{7,4},{8,9},{9,10},{10,1... | collective-permute-start | bytes 245768 | tf_op jit(solution)/shard_map/ppermute | solution.py:21
  19.8 2.1 %collective-permute-start.3 = (bf16[4,10,4,256]{3,2,1,0:T(4,128)(2,1)S(1)}, bf16[4,10,4,256]{3,2,1,0:T(4,128)(2,1)S(1)}, u32[]{:S(2)}, u32[]{:S(2)}) collective-permute-start(bf16[4,10,4,256]{3,2,1,0:T(4,128)(2,1)S(1)} %get-tuple-element.202), channel_id=1, source_target_pairs={{1,0},{2,1},{3,2},{0,3},{5,4},{6,5},{7,6},{4,7},{9,8},{10,9},{11,1... | collective-permute-start | bytes 245768 | tf_op jit(solution)/shard_map/ppermute | solution.py:24
  21.9 0.3 convolution_select_fusion
  22.3 0.3 copy.22
  22.5 2.4 %collective-permute-done.2 = bf16[4,10,4,256]{3,2,1,0:T(4,128)(2,1)S(1)} collective-permute-done((bf16[4,10,4,256]{3,2,1,0:T(4,128)(2,1)S(1)}, bf16[4,10,4,256]{3,2,1,0:T(4,128)(2,1)S(1)}, u32[]{:S(2)}, u32[]{:S(2)}) %collective-permute-start.2) | collective-permute-done | bytes 81952 | tf_op jit(solution)/shard_map/ppermute | solution.py:21
  24.9 1.9 %collective-permute-done.3 = bf16[4,10,4,256]{3,2,1,0:T(4,128)(2,1)S(1)} collective-permute-done((bf16[4,10,4,256]{3,2,1,0:T(4,128)(2,1)S(1)}, bf16[4,10,4,256]{3,2,1,0:T(4,128)(2,1)S(1)}, u32[]{:S(2)}, u32[]{:S(2)}) %collective-permute-start.3) | collective-permute-done | bytes 81952 | tf_op jit(solution)/shard_map/ppermute | solution.py:24
  26.8 0.3 pad_maximum_fusion
  27.1 2.4 %broadcast.874.clone = bf16[4,8,16,9,256]{4,3,2,1,0:T(8,128)(2,1)} broadcast(bf16[]{:T(256)} %constant.17.clone.1), dimensions={} | broadcast | bytes 2359298 | tf_op jit(solution)/shard_map/broadcast.10
  29.5 25.8 %while.20 = (s32[]{:T(128)}, bf16[4,8,16,9,256]{4,3,2,1,0:T(8,128)(2,1)}, f32[8,9,3,9]{1,0,3,2:T(8,128)S(1)}, bf16[4,10,24,256]{3,2,1,0:T(8,128)(2,1)S(1)}, s32[]{:T(128)}) while((s32[]{:T(128)}, bf16[4,8,16,9,256]{4,3,2,1,0:T(8,128)(2,1)}, f32[8,9,3,9]{1,0,3,2:T(8,128)S(1)}, bf16[4,10,24,256]{3,2,1,0:T(8,128)(2,1)S(1)}, s32[]{:T(128)}) %tuple.162), condition=%wide.region_3.4_spmd, body=%wide.region_2.3_spmd.sunk | while | flops 16809984 | bytes 10165101 | solution.py:78
  29.6 0.1 slice_convert_fusion.59
  29.7 0.3 slice_convert_fusion.58
  30.0 6.0 %fusion.40 = bf16[4,8,16,9,256]{4,3,2,1,0:T(8,128)(2,1)} fusion(bf16[4,8,16,9,256]{4,3,2,1,0:T(8,128)(2,1)} %get-tuple-element.479, s32[]{:T(128)S(6)} %copy.43, f32[8,16,256]{2,1,0:T(8,128)S(1)} %get-tuple-element.361, f32[8,9]{1,0:T(8,128)S(1)} %get-tuple-element.362, f32[8,16,256]{2,1,0:T(8,128)S(1)} %get-tuple-element.363, ...), kind=kLoop, calls=%fused_computation.1.clone.1 | loop fusion | flops 15925248 | bytes 4595300 | tf_op jit(solution)/shard_map/while/body/jit(dynamic_update_index_in_dim)/dynamic_update_slice | solution.py:78
  36.0 0.1 slice_convert_fusion.59
  36.1 0.3 slice_convert_fusion.58
  36.4 6.0 %fusion.40 = bf16[4,8,16,9,256]{4,3,2,1,0:T(8,128)(2,1)} fusion(bf16[4,8,16,9,256]{4,3,2,1,0:T(8,128)(2,1)} %get-tuple-element.479, s32[]{:T(128)S(6)} %copy.43, f32[8,16,256]{2,1,0:T(8,128)S(1)} %get-tuple-element.361, f32[8,9]{1,0:T(8,128)S(1)} %get-tuple-element.362, f32[8,16,256]{2,1,0:T(8,128)S(1)} %get-tuple-element.363, ...), kind=kLoop, calls=%fused_computation.1.clone.1 | loop fusion | flops 15925248 | bytes 4595300 | tf_op jit(solution)/shard_map/while/body/jit(dynamic_update_index_in_dim)/dynamic_update_slice | solution.py:78
  42.4 0.1 slice_convert_fusion.59
  42.6 0.3 slice_convert_fusion.58
  42.9 6.0 %fusion.40 = bf16[4,8,16,9,256]{4,3,2,1,0:T(8,128)(2,1)} fusion(bf16[4,8,16,9,256]{4,3,2,1,0:T(8,128)(2,1)} %get-tuple-element.479, s32[]{:T(128)S(6)} %copy.43, f32[8,16,256]{2,1,0:T(8,128)S(1)} %get-tuple-element.361, f32[8,9]{1,0:T(8,128)S(1)} %get-tuple-element.362, f32[8,16,256]{2,1,0:T(8,128)S(1)} %get-tuple-element.363, ...), kind=kLoop, calls=%fused_computation.1.clone.1 | loop fusion | flops 15925248 | bytes 4595300 | tf_op jit(solution)/shard_map/while/body/jit(dynamic_update_index_in_dim)/dynamic_update_slice | solution.py:78
  48.9 0.1 slice_convert_fusion.59
  49.0 0.3 slice_convert_fusion.58
  49.3 6.0 %fusion.40 = bf16[4,8,16,9,256]{4,3,2,1,0:T(8,128)(2,1)} fusion(bf16[4,8,16,9,256]{4,3,2,1,0:T(8,128)(2,1)} %get-tuple-element.479, s32[]{:T(128)S(6)} %copy.43, f32[8,16,256]{2,1,0:T(8,128)S(1)} %get-tuple-element.361, f32[8,9]{1,0:T(8,128)S(1)} %get-tuple-element.362, f32[8,16,256]{2,1,0:T(8,128)S(1)} %get-tuple-element.363, ...), kind=kLoop, calls=%fused_computation.1.clone.1 | loop fusion | flops 15925248 | bytes 4595300 | tf_op jit(solution)/shard_map/while/body/jit(dynamic_update_index_in_dim)/dynamic_update_slice | solution.py:78
  55.3 3.5 %copy.26 = bf16[64,8,9,256]{3,1,2,0:T(8,128)(2,1)S(1)} copy(bf16[64,8,9,256]{3,2,1,0:T(8,128)(2,1)} %bitcast.159) | data formatting | bytes 4718592
  58.8 1.8 %fusion.20 = (bf16[512,256]{1,0:T(8,128)(2,1)S(1)}, bf16[512,256]{1,0:T(8,128)(2,1)}) fusion(bf16[4,8,16,256]{3,2,1,0:T(8,128)(2,1)S(1)} %copy-done.3, bf16[4,8,16,256]{3,2,1,0:T(8,128)(2,1)S(1)} %copy-done.2, bf16[512,2304]{1,0:T(8,128)(2,1)S(1)} %bitcast.161, bf16[2304,256]{1,0:T(8,128)(2,1)S(1)} %bitcast.158), kind=kOutput, calls=%fused_computation.132 | convolution fusion | flops 607256576 | bytes 4587520 | tf_op jit(solution)/shard_map/dot_general | solution.py:117
  60.7 1.9 %collective-permute-start.4 = (bf16[4,1,16,256]{3,2,1,0:T(8,128)(2,1)S(1)}, bf16[4,1,16,256]{3,2,1,0:T(8,128)(2,1)S(1)}, u32[]{:S(2)}, u32[]{:S(2)}) collective-permute-start(bf16[4,1,16,256]{3,2,1,0:T(8,128)(2,1)S(1)} %get-tuple-element.203), channel_id=1, source_target_pairs={{0,4},{4,8},{8,12},{1,5},{5,9},{9,13},{2,6},{6,10},{10,14},{3,7},{... | collective-permute-start | bytes 98312 | tf_op jit(solution)/shard_map/ppermute | solution.py:21
  62.6 1.3 collective-permute-start.5
  63.9 0.4 copy.23
  64.3 1.4 collective-permute-done.5
  65.7 0.1 pad_maximum_fusion.4
  65.8 0.8 collective-permute-start.6
  66.6 3.1 %collective-permute-start.7 = (bf16[4,10,4,256]{3,2,1,0:T(4,128)(2,1)S(1)}, bf16[4,10,4,256]{3,2,1,0:T(4,128)(2,1)S(1)}, u32[]{:S(2)}, u32[]{:S(2)}) collective-permute-start(bf16[4,10,4,256]{3,2,1,0:T(4,128)(2,1)S(1)} %get-tuple-element.200), channel_id=1, source_target_pairs={{1,0},{2,1},{3,2},{0,3},{5,4},{6,5},{7,6},{4,7},{9,8},{10,9},{11,1... | collective-permute-start | bytes 245768 | tf_op jit(solution)/shard_map/ppermute | solution.py:24
  69.6 3.5 %fusion.2 = bf16[2304,256]{1,0:T(8,128)(2,1)} fusion(bf16[512,2304]{1,0:T(8,128)(2,1)} %bitcast.162, bf16[512,256]{1,0:T(8,128)(2,1)S(1)} %get-tuple-element.197), kind=kOutput, calls=%fused_computation.115 | convolution fusion | flops 605159424 | bytes 3801088 | tf_op jit(solution)/shard_map/dot_general | solution.py:130
  73.2 0.0 all-reduce.2.cloned.1.call-start
  73.3 0.3 pad_maximum_fusion.1
  73.6 2.4 %broadcast.874 = bf16[4,8,16,9,256]{4,3,2,1,0:T(8,128)(2,1)} broadcast(bf16[]{:T(256)} %constant.17.clone.1), dimensions={} | broadcast | bytes 2359298 | tf_op jit(solution)/shard_map/broadcast.10
  76.0 25.5 %while.21 = (s32[]{:T(128)}, bf16[4,8,16,9,256]{4,3,2,1,0:T(8,128)(2,1)}, f32[10,9,3,9]{1,0,3,2:T(8,128)S(1)}, bf16[4,10,24,256]{3,2,1,0:T(8,128)(2,1)S(1)}, s32[]{:T(128)}) while((s32[]{:T(128)}, bf16[4,8,16,9,256]{4,3,2,1,0:T(8,128)(2,1)}, f32[10,9,3,9]{1,0,3,2:T(8,128)S(1)}, bf16[4,10,24,256]{3,2,1,0:T(8,128)(2,1)S(1)}, s32[]{:T(128)}) %tuple.165), condition=%wide.region_5.6_spmd, body=%wide.region_4.5_spmd.sunk | while | flops 16809984 | bytes 10165101 | solution.py:100
  76.0 0.1 slice_convert_fusion.61
  76.2 0.3 slice_convert_fusion.60
  76.5 5.9 %fusion.41 = bf16[4,8,16,9,256]{4,3,2,1,0:T(8,128)(2,1)} fusion(bf16[4,8,16,9,256]{4,3,2,1,0:T(8,128)(2,1)} %get-tuple-element.494, s32[]{:T(128)S(6)} %copy.49, f32[8,16,256]{2,1,0:T(8,128)S(1)} %get-tuple-element.419, f32[8,9]{1,0:T(8,128)S(1)} %get-tuple-element.420, f32[8,16,256]{2,1,0:T(8,128)S(1)} %get-tuple-element.421, ...), kind=kLoop, calls=%fused_computation.58.clone.1 | loop fusion | flops 15925248 | bytes 4595300 | tf_op jit(solution)/shard_map/while/body/jit(dynamic_update_index_in_dim)/dynamic_update_slice | solution.py:78
  82.4 0.1 slice_convert_fusion.61
  82.5 0.3 slice_convert_fusion.60
  82.8 5.9 %fusion.41 = bf16[4,8,16,9,256]{4,3,2,1,0:T(8,128)(2,1)} fusion(bf16[4,8,16,9,256]{4,3,2,1,0:T(8,128)(2,1)} %get-tuple-element.494, s32[]{:T(128)S(6)} %copy.49, f32[8,16,256]{2,1,0:T(8,128)S(1)} %get-tuple-element.419, f32[8,9]{1,0:T(8,128)S(1)} %get-tuple-element.420, f32[8,16,256]{2,1,0:T(8,128)S(1)} %get-tuple-element.421, ...), kind=kLoop, calls=%fused_computation.58.clone.1 | loop fusion | flops 15925248 | bytes 4595300 | tf_op jit(solution)/shard_map/while/body/jit(dynamic_update_index_in_dim)/dynamic_update_slice | solution.py:78
  88.8 0.1 slice_convert_fusion.61
  88.9 0.3 slice_convert_fusion.60
  89.2 5.9 %fusion.41 = bf16[4,8,16,9,256]{4,3,2,1,0:T(8,128)(2,1)} fusion(bf16[4,8,16,9,256]{4,3,2,1,0:T(8,128)(2,1)} %get-tuple-element.494, s32[]{:T(128)S(6)} %copy.49, f32[8,16,256]{2,1,0:T(8,128)S(1)} %get-tuple-element.419, f32[8,9]{1,0:T(8,128)S(1)} %get-tuple-element.420, f32[8,16,256]{2,1,0:T(8,128)S(1)} %get-tuple-element.421, ...), kind=kLoop, calls=%fused_computation.58.clone.1 | loop fusion | flops 15925248 | bytes 4595300 | tf_op jit(solution)/shard_map/while/body/jit(dynamic_update_index_in_dim)/dynamic_update_slice | solution.py:78
  95.1 0.1 slice_convert_fusion.61
  95.3 0.3 slice_convert_fusion.60
  95.6 5.9 %fusion.41 = bf16[4,8,16,9,256]{4,3,2,1,0:T(8,128)(2,1)} fusion(bf16[4,8,16,9,256]{4,3,2,1,0:T(8,128)(2,1)} %get-tuple-element.494, s32[]{:T(128)S(6)} %copy.49, f32[8,16,256]{2,1,0:T(8,128)S(1)} %get-tuple-element.419, f32[8,9]{1,0:T(8,128)S(1)} %get-tuple-element.420, f32[8,16,256]{2,1,0:T(8,128)S(1)} %get-tuple-element.421, ...), kind=kLoop, calls=%fused_computation.58.clone.1 | loop fusion | flops 15925248 | bytes 4595300 | tf_op jit(solution)/shard_map/while/body/jit(dynamic_update_index_in_dim)/dynamic_update_slice | solution.py:78
  101.5 0.6 reduce-scatter.2.cloned.1.call-done
  102.1 4.4 %fusion.11 = bf16[512,256]{1,0:T(8,128)(2,1)} fusion(bf16[9,256,256]{2,1,0:T(8,128)(2,1)S(1)} %copy-done, bf16[512,9,256]{2,1,0:T(8,128)(2,1)} %bitcast.160, bf16[512,256]{1,0:T(8,128)(2,1)S(1)} %bitcast.168), kind=kOutput, calls=%fused_computation.120 | convolution fusion | flops 604372992 | bytes 4063232 | tf_op jit(solution)/shard_map/dot_general | solution.py:140
  106.4 50.6 %all-reduce.2.cloned.1.call-done = bf16[9,64,256]{2,1,0:T(8,128)(2,1)} async-done(((bf16[9,64,256]{2,1,0:T(8,128)(2,1)}), bf16[9,64,256]{2,1,0:T(8,128)(2,1)}) %all-reduce.2.cloned.1.call-update) | async-done | bytes 294928 | tf_op jit(solution)/shard_map/psum | solution.py:137
  157.0 1.8 %convert_element_type.284 = f32[9,64,256]{2,1,0:T(8,128)} convert(bf16[9,64,256]{2,1,0:T(8,128)(2,1)} %all-reduce.2.cloned.1.call-done) | non-fusion elementwise | flops 147456 | bytes 884736 | tf_op jit(solution)/shard_map/convert_element_type | solution.py:137
  (46 shorter events, 0.4 us)
Async XLA Ops:
  7.2 51.6 %copy-start = (bf16[9,256,256]{2,1,0:T(8,128)(2,1)S(1)}, bf16[9,256,256]{2,1,0:T(8,128)(2,1)}, u32[]{:S(2)}) copy-start(bf16[9,256,256]{2,1,0:T(8,128)(2,1)} %param.12) | copy-start | bytes 3538948
  7.2 94.9 %reduce-scatter.2.cloned.1.call-start = ((), (), s32[]{:S(2)}) async-start(), calls=%async_computation.1 | async-start | bytes 1474560 | tf_op jit(solution)/shard_map/reduce_scatter | solution.py:134
  8.1 8.6 %collective-permute-start.1 = (bf16[4,1,16,256]{3,2,1,0:T(8,128)(2,1)S(1)}, bf16[4,1,16,256]{3,2,1,0:T(8,128)(2,1)S(1)}, u32[]{:S(2)}, u32[]{:S(2)}) collective-permute-start(bf16[4,1,16,256]{3,2,1,0:T(8,128)(2,1)S(1)} %get-tuple-element.205), channel_id=1, source_target_pairs={{4,0},{8,4},{12,8},{5,1},{9,5},{13,9},{6,2},{10,6},{14,10},{7,3},{... | collective-permute-start | bytes 98312 | tf_op jit(solution)/shard_map/ppermute | solution.py:24
  9.4 6.3 %collective-permute-start = (bf16[4,1,16,256]{3,2,1,0:T(8,128)(2,1)S(1)}, bf16[4,1,16,256]{3,2,1,0:T(8,128)(2,1)S(1)}, u32[]{:S(2)}, u32[]{:S(2)}) collective-permute-start(bf16[4,1,16,256]{3,2,1,0:T(8,128)(2,1)S(1)} %get-tuple-element.206), channel_id=1, source_target_pairs={{0,4},{4,8},{8,12},{1,5},{5,9},{9,13},{2,6},{6,10},{10,14},{3,7},{... | collective-permute-start | bytes 98312 | tf_op jit(solution)/shard_map/ppermute | solution.py:21
  16.8 8.2 %collective-permute-start.2 = (bf16[4,10,4,256]{3,2,1,0:T(4,128)(2,1)S(1)}, bf16[4,10,4,256]{3,2,1,0:T(4,128)(2,1)S(1)}, u32[]{:S(2)}, u32[]{:S(2)}) collective-permute-start(bf16[4,10,4,256]{3,2,1,0:T(4,128)(2,1)S(1)} %get-tuple-element.201), channel_id=1, source_target_pairs={{0,1},{1,2},{2,3},{3,0},{4,5},{5,6},{6,7},{7,4},{8,9},{9,10},{10,1... | collective-permute-start | bytes 245768 | tf_op jit(solution)/shard_map/ppermute | solution.py:21
  19.8 7.0 %collective-permute-start.3 = (bf16[4,10,4,256]{3,2,1,0:T(4,128)(2,1)S(1)}, bf16[4,10,4,256]{3,2,1,0:T(4,128)(2,1)S(1)}, u32[]{:S(2)}, u32[]{:S(2)}) collective-permute-start(bf16[4,10,4,256]{3,2,1,0:T(4,128)(2,1)S(1)} %get-tuple-element.202), channel_id=1, source_target_pairs={{1,0},{2,1},{3,2},{0,3},{5,4},{6,5},{7,6},{4,7},{9,8},{10,9},{11,1... | collective-permute-start | bytes 245768 | tf_op jit(solution)/shard_map/ppermute | solution.py:24
  55.3 3.5 %copy-start.2 = (bf16[4,8,16,256]{3,2,1,0:T(8,128)(2,1)S(1)}, bf16[4,8,16,256]{3,2,1,0:T(8,128)(2,1)}, u32[]{:S(2)}) copy-start(bf16[4,8,16,256]{3,2,1,0:T(8,128)(2,1)} %param.10) | copy-start | bytes 786436
  55.3 3.5 %copy-start.3 = (bf16[4,8,16,256]{3,2,1,0:T(8,128)(2,1)S(1)}, bf16[4,8,16,256]{3,2,1,0:T(8,128)(2,1)}, u32[]{:S(2)}) copy-start(bf16[4,8,16,256]{3,2,1,0:T(8,128)(2,1)} %param.11) | copy-start | bytes 786436
  58.8 1.8 %copy-start.1 = (bf16[64,8,9,256]{3,1,2,0:T(8,128)(2,1)}, bf16[64,8,9,256]{3,1,2,0:T(8,128)(2,1)S(1)}, u32[]{:S(2)}) copy-start(bf16[64,8,9,256]{3,1,2,0:T(8,128)(2,1)S(1)} %copy.26) | copy-start | bytes 7077892
  60.7 3.6 %collective-permute-start.4 = (bf16[4,1,16,256]{3,2,1,0:T(8,128)(2,1)S(1)}, bf16[4,1,16,256]{3,2,1,0:T(8,128)(2,1)S(1)}, u32[]{:S(2)}, u32[]{:S(2)}) collective-permute-start(bf16[4,1,16,256]{3,2,1,0:T(8,128)(2,1)S(1)} %get-tuple-element.203), channel_id=1, source_target_pairs={{0,4},{4,8},{8,12},{1,5},{5,9},{9,13},{2,6},{6,10},{10,14},{3,7},{... | collective-permute-start | bytes 98312 | tf_op jit(solution)/shard_map/ppermute | solution.py:21
  62.6 3.1 %collective-permute-start.5 = (bf16[4,1,16,256]{3,2,1,0:T(8,128)(2,1)S(1)}, bf16[4,1,16,256]{3,2,1,0:T(8,128)(2,1)S(1)}, u32[]{:S(2)}, u32[]{:S(2)}) collective-permute-start(bf16[4,1,16,256]{3,2,1,0:T(8,128)(2,1)S(1)} %get-tuple-element.204), channel_id=1, source_target_pairs={{4,0},{8,4},{12,8},{5,1},{9,5},{13,9},{6,2},{10,6},{14,10},{7,3},{... | collective-permute-start | bytes 98312 | tf_op jit(solution)/shard_map/ppermute | solution.py:24
  65.8 7.5 %collective-permute-start.6 = (bf16[4,10,4,256]{3,2,1,0:T(4,128)(2,1)S(1)}, bf16[4,10,4,256]{3,2,1,0:T(4,128)(2,1)S(1)}, u32[]{:S(2)}, u32[]{:S(2)}) collective-permute-start(bf16[4,10,4,256]{3,2,1,0:T(4,128)(2,1)S(1)} %get-tuple-element.199), channel_id=1, source_target_pairs={{0,1},{1,2},{2,3},{3,0},{4,5},{5,6},{6,7},{7,4},{8,9},{9,10},{10,1... | collective-permute-start | bytes 245768 | tf_op jit(solution)/shard_map/ppermute | solution.py:21
  66.6 6.7 %collective-permute-start.7 = (bf16[4,10,4,256]{3,2,1,0:T(4,128)(2,1)S(1)}, bf16[4,10,4,256]{3,2,1,0:T(4,128)(2,1)S(1)}, u32[]{:S(2)}, u32[]{:S(2)}) collective-permute-start(bf16[4,10,4,256]{3,2,1,0:T(4,128)(2,1)S(1)} %get-tuple-element.200), channel_id=1, source_target_pairs={{1,0},{2,1},{3,2},{0,3},{5,4},{6,5},{7,6},{4,7},{9,8},{10,9},{11,1... | collective-permute-start | bytes 245768 | tf_op jit(solution)/shard_map/ppermute | solution.py:24
  73.2 83.8 %all-reduce.2.cloned.1.call-start = ((), (), s32[]{:S(2)}) async-start(), calls=%async_computation.2 | async-start | bytes 589824 | tf_op jit(solution)/shard_map/psum | solution.py:137
Sparse Core Ops, SparseCore 0:
  73.3 28.6 reduce-scatter.1
  105.2 51.7 all-reduce.1
where the time goes:
time: 166 us
  waiting for transfers between devices  56.9 us (34%)
  other arithmetic  55.2 us (33%)
  starting transfers between devices  16.6 us (10%)
  between operations  14.3 us (9%)
  local copies, waits for them, and re-layouts  12.5 us (8%)
  matrix products  10 us (6%)
    psum x1, waiting for transfers between devices, shards(): weight_grad = lax.psum(share_grad, ('ens', 'lat')).astype(jnp.float32)  50.6 us
    dynamic_update_slice x8, other arithmetic, spread_forward(): return lax.map(single, padded)  47.4 us
    ppermute x4, starting transfers between devices, extended(): lax.ppermute(lax.slice_in_dim(block, block.shape[dim] - width, None, axis...  8.82 us
    ppermute x4, starting transfers between devices, extended(): lax.ppermute(lax.slice_in_dim(block, 0, width, axis=dim), axis, backward)  7.74 us
    unnamed x12, local copies, waits for them, and re-layouts  5.44 us
    another operation x2, local copies, waits for them, and re-layouts  4.84 us
    dot_general x1, matrix products, shards(): lax.dot_general(back.reshape(-1, K, C), weight, (((1, 2), (0, 2)), ((), (...  4.36 us
    dot_general x1, matrix products, shards(): lax.dot_general(feature_rows, grad_mixed, (((0,), (0,)), ((), ())), prefe...  3.54 us
  transfers between devices with their start and end apart: 10, of which 5 were waited for; matrix products, arithmetic and copies ran while one was open for 25% of the time, Pallas kernels for 0%

commit v1 on v0

v1 whole, which is shorter than its diff:
```python
import functools
import math

import jax
import jax.numpy as jnp
import numpy as np
from jax import lax
from jax.experimental import pallas as pl
from jax.experimental.pallas import tpu as pltpu
from jax.sharding import PartitionSpec as P

R = 1
H = 4
MESH = pl.DeviceIdType.MESH
BF = jnp.bfloat16
F32 = jnp.float32


def layout(members, rows, cols):
    cells = [(i, j) for i in range(rows) for j in range(cols)]
    cells += [(-1, j) for j in range(cols)] + [(rows, j) for j in range(cols)]
    cells += [(i, j - H) for i in range(rows) for j in range(H)]
    cells += [(i, cols + j) for i in range(rows) for j in range(H)]
    for i in (-1, rows):
        for first in (-H, cols):
            cells += [(i, first + j) for j in range(H)]
    depth = -(-len(cells) // 128) * 128
    pos = np.full((8, depth), -1000, np.int32)
    for p, (i, j) in enumerate(cells):
        pos[0, p], pos[1, p] = i, j
    own = rows * cols
    index = lambda m, i, j: m * own + i * cols + j
    picks = [index(m, i, j) for m in range(members) for i in range(rows) for j in range(H)]
    picks += [
        index(m, i, cols - H + j) for m in range(members) for i in range(rows) for j in range(H)
    ]
    for i in (0, rows - 1):
        for first in (0, cols - H):
            picks += [index(m, i, first + j) for m in range(members) for j in range(H)]
    select = np.zeros((len(picks), members * own), np.float32)
    select[np.arange(len(picks)), picks] = 1
    corners = 4 * members * H
    regroup = np.zeros((corners, corners), np.float32)
    for m in range(members):
        for q in range(4):
            for j in range(H):
                regroup[(m * 4 + q) * H + j, (q * members + m) * H + j] = 1
    return len(cells), depth, pos, select, regroup


def block_kernel(
    dims,
    x_hbm, og_hbm, w_hbm, basis_ref, cb_ref, hw_ref, pos_ref, reach_ref, select_ref, regroup_ref,
    res_hbm, ing_hbm, wg_hbm,
    xp, gp, og, w, feats, fwd, adj, packs, crecv, res, ing, wg, lsem, ssem, rsem,
):
    members, rows, cols, chan, basis, used, depth, lats, lons, total, scale = dims
    own = rows * cols
    rim = rows * H
    taps = 2 * H + 1
    lat = lax.axis_index("lat")
    lon = lax.axis_index("lon")
    west = lax.rem(lon + lons - 1, lons)
    east = lax.rem(lon + 1, lons)
    has_n = lat > 0
    has_s = lat < lats - 1

    load_x = pltpu.make_async_copy(x_hbm, xp.at[:, pl.ds(0, own), :], lsem.at[0])
    load_x.start()
    load_og = pltpu.make_async_copy(og_hbm, og, lsem.at[1])
    load_og.start()
    load_w = pltpu.make_async_copy(w_hbm, w, lsem.at[2])
    load_w.start()

    barrier = pltpu.get_barrier_semaphore()

    def greet(where):
        pl.semaphore_signal(barrier, inc=1, device_id=where, device_id_type=MESH)

    greet({"lon": west})
    greet({"lon": east})

    @pl.when(has_n)
    def _():
        for z in (lon, west, east):
            greet({"lat": lat - 1, "lon": z})

    @pl.when(has_s)
    def _():
        for z in (lon, west, east):
            greet({"lat": lat + 1, "lon": z})

    def clear(pad, land):
        pad[:, used:, :] = jnp.zeros((members, depth - used, chan), BF)

        @pl.when(jnp.logical_not(has_n))
        def _():
            pad[:, own : own + cols, :] = jnp.zeros((members, cols, chan), BF)
            land[0:2] = jnp.zeros((2,) + land.shape[1:], BF)

        @pl.when(jnp.logical_not(has_s))
        def _():
            pad[:, own + cols : own + 2 * cols, :] = jnp.zeros((members, cols, chan), BF)
            land[2:4] = jnp.zeros((2,) + land.shape[1:], BF)

    wide = members * rim
    mh = members * H

    def copies(t):
        pad = (xp, gp)[t]
        pack = packs.at[t]
        land = crecv.at[t]
        top, bottom = pl.ds(own, cols), pl.ds(own + cols, cols)
        left, right = pl.ds(own + 2 * cols, rim), pl.ds(own + 2 * cols + rim, rim)
        corner = lambda q: pack.at[pl.ds(2 * wide + q * mh, mh)]
        north, south = {"lat": lat - 1}, {"lat": lat + 1}
        plan = [
            (pad.at[:, pl.ds(0, cols), :], pad.at[:, bottom, :], north),
            (pad.at[:, pl.ds(own - cols, cols), :], pad.at[:, top, :], south),
            (None, right, {"lon": west}),
            (None, left, {"lon": east}),
            (corner(0), land.at[3], {"lat": lat - 1, "lon": west}),
            (corner(1), land.at[2], {"lat": lat - 1, "lon": east}),
            (corner(2), land.at[1], {"lat": lat + 1, "lon": west}),
            (corner(3), land.at[0], {"lat": lat + 1, "lon": east}),
        ]
        out = {}
        slot = 0
        for q, (src, dst, where) in enumerate(plan):
            if src is None:
                parts = [
                    (pack.at[pl.ds((q - 2) * wide + m * rim, rim)], pad.at[m, dst, :])
                    for m in range(members)
                ]
            else:
                parts = [(src, dst)]
            out[q] = []
            for a, b in parts:
                out[q].append(
                    pltpu.make_async_remote_copy(
                        src_ref=a, dst_ref=b, send_sem=ssem.at[t, slot], recv_sem=rsem.at[t, slot],
                        device_id=where, device_id_type=MESH,
                    )
                )
                slot += 1
        return out

    NORTH, SOUTH, SIDES = (0, 4, 5), (1, 6, 7), (2, 3)

    def each(c, qs, act):
        for q in qs:
            for one in c[q]:
                act(one)

    def send(t):
        c = copies(t)
        pad = (xp, gp)[t]

        flat = pad[:, :own, :].reshape(members * own, chan)
        packs[t] = jnp.dot(select_ref[...], flat, preferred_element_type=F32).astype(BF)
        each(c, SIDES, lambda one: one.start())

        @pl.when(has_n)
        def _():
            each(c, NORTH, lambda one: one.start())

        @pl.when(has_s)
        def _():
            each(c, SOUTH, lambda one: one.start())

    def receive(t):
        c = copies(t)
        pad = (xp, gp)[t]

        each(c, SIDES, lambda one: one.wait_recv())

        @pl.when(has_s)
        def _():
            each(c, NORTH, lambda one: one.wait_recv())

        @pl.when(has_n)
        def _():
            each(c, SOUTH, lambda one: one.wait_recv())

        got = jnp.dot(
            regroup_ref[...], crecv[t].reshape(4 * mh, chan), preferred_element_type=F32
        ).astype(BF)
        for m in range(members):
            pad[m, used - 4 * H : used, :] = got[m * 4 * H : (m + 1) * 4 * H]

    def sent(t):
        c = copies(t)
        each(c, SIDES, lambda one: one.wait_send())

        @pl.when(has_n)
        def _():
            each(c, NORTH, lambda one: one.wait_send())

        @pl.when(has_s)
        def _():
            each(c, SOUTH, lambda one: one.wait_send())

    clear(xp, crecv.at[0])
    clear(gp, crecv.at[1])
    load_x.wait()
    pl.semaphore_wait(
        barrier, 2 + 3 * has_n.astype(jnp.int32) + 3 * has_s.astype(jnp.int32)
    )
    send(0)

    lane = lax.broadcasted_iota(jnp.int32, reach_ref.shape, 1)
    first = lat * rows
    cell_i, cell_j = pos_ref[0:1, :], pos_ref[1:2, :]
    step = lax.broadcasted_iota(jnp.int32, (128, depth), 0)
    col = lax.broadcasted_iota(jnp.int32, (cols, depth), 0)
    ahead = cell_j - col + H
    behind = col - cell_j + H

    def filters(i):
        cyc = jnp.clip(first + i, 0, total - 1)
        table = basis_ref[cb_ref[cyc]]
        span = jnp.where(
            lane == 0, hw_ref[cyc, 0], jnp.where(lane == 1, hw_ref[cyc, 1], hw_ref[cyc, 2])
        )
        return jnp.where(reach_ref[...] <= span, table, 0.0)

    def expand(table, rowsel, offset, dst, i):
        spread = jnp.dot(table.astype(BF), rowsel.astype(BF), preferred_element_type=F32)
        for k in range(basis):
            acc = jnp.zeros((cols, depth), F32)
            for d in range(taps):
                line = spread[k * taps + d : k * taps + d + 1, :]
                acc = jnp.where(offset == d, line, acc)
            dst[pl.ds(pl.multiple_of(k * own + i * cols, cols), cols), :] = acc.astype(BF)

    def build(i, carry):
        here = filters(i)
        onward = jnp.where(cell_i - i + R == step, 1.0, 0.0)
        expand(here, onward, ahead, fwd, i)
        table = jnp.where(
            lane == 0, filters(i + 1), jnp.where(lane == 1, here, filters(i - 1))
        )
        back = jnp.where(i + R - cell_i == step, 1.0, 0.0)
        expand(jnp.where(lane < 3, table, 0.0), back, behind, adj, i)
        return carry

    lax.fori_loop(0, rows, build, 0)

    def spread_all(mat, pad):
        def one(m, carry):
            block = pad[m]
            at = pl.ds(pl.multiple_of(m * own, own), own)
            for k in range(basis):
                feats[at, k * chan : (k + 1) * chan] = jnp.dot(
                    mat[k * own : (k + 1) * own, :], block, preferred_element_type=F32
                ).astype(BF)
            return carry

        lax.fori_loop(0, members, one, 0)

    receive(0)
    spread_all(fwd, xp)
    load_w.wait()
    load_og.wait()

    def forward(m, carry):
        at = pl.ds(pl.multiple_of(m * own, own), own)
        v = jnp.dot(
            feats[at, :], w[...].reshape(basis * chan, chan), preferred_element_type=F32
        )
        root = math.sqrt(2.0 / math.pi)
        vv = v * v
        th = jnp.tanh(root * (v + 0.044715 * (vv * v)))
        half = 0.5 * (1.0 + th)
        res[m] = (xp[m, :own, :].astype(F32) + v * half).astype(BF)
        slope = half + 0.5 * v * (1.0 - th * th) * (root * (1.0 + 3 * 0.044715 * vv))
        gp[m, :own, :] = (og[m].astype(F32) * slope).astype(BF)
        return carry

    lax.fori_loop(0, members, forward, 0)
    send(1)
    save_res = pltpu.make_async_copy(res, res_hbm, lsem.at[3])
    save_res.start()

    grad = gp[:, :own, :].reshape(members * own, chan)
    for k in range(basis):
        part = lax.dot_general(
            feats[:, k * chan : (k + 1) * chan], grad, (((0,), (0,)), ((), ())),
            preferred_element_type=F32,
        )
        wg[k] = (part * scale).astype(BF)
    save_wg = pltpu.make_async_copy(wg, wg_hbm, lsem.at[4])
    save_wg.start()

    receive(1)
    spread_all(adj, gp)

    def backward(m, carry):
        at = pl.ds(pl.multiple_of(m * own, own), own)
        acc = og[m].astype(F32)
        for k in range(basis):
            acc = acc + lax.dot_general(
                feats[at, k * chan : (k + 1) * chan], w[k], (((1,), (1,)), ((), ())),
                preferred_element_type=F32,
            )
        ing[m] = acc.astype(BF)
        return carry

    lax.fori_loop(0, members, backward, 0)
    save_ing = pltpu.make_async_copy(ing, ing_hbm, lsem.at[5])
    save_ing.start()
    sent(0)
    sent(1)
    save_res.wait()
    save_wg.wait()
    save_ing.wait()


def shards(members_in, out_grad, weight, basis_blocks, cycle_block, half_width):
    members, rows, cols, chan = members_in.shape
    blocks, basis, reach, taps = basis_blocks.shape
    own = rows * cols
    lats, lons = lax.axis_size("lat"), lax.axis_size("lon")
    used, depth, pos, select, regroup = layout(members, rows, cols)
    lines = -(-basis * taps // 16) * 16
    table = jnp.transpose(basis_blocks, (0, 1, 3, 2)).reshape(blocks, basis * taps, reach)
    table = jnp.pad(table, ((0, 0), (0, lines - basis * taps), (0, 128 - reach)))
    far = np.broadcast_to(np.abs(np.arange(lines) % taps - H)[:, None], (lines, 128))
    cell_count = members * lax.axis_size("ens") * own * lats * lons
    dims = (
        members, rows, cols, chan, basis, used, depth, lats, lons, cycle_block.shape[0],
        1.0 / math.sqrt(cell_count),
    )
    anywhere = pl.BlockSpec(memory_space=pl.ANY)
    vmem = pl.BlockSpec(memory_space=pltpu.VMEM)
    smem = pl.BlockSpec(memory_space=pltpu.SMEM)
    cells = (members, own, chan)
    padded = (members, depth, chan)
    slots = 6 + 2 * members
    res, ing, local_grad = pl.pallas_call(
        functools.partial(block_kernel, dims),
        out_shape=[
            jax.ShapeDtypeStruct(cells, BF),
            jax.ShapeDtypeStruct(cells, BF),
            jax.ShapeDtypeStruct((basis, chan, chan), BF),
        ],
        in_specs=[anywhere] * 3 + [vmem, smem, smem] + [vmem] * 4,
        out_specs=[anywhere] * 3,
        scratch_shapes=[
            pltpu.VMEM(padded, BF),
            pltpu.VMEM(padded, BF),
            pltpu.VMEM(cells, BF),
            pltpu.VMEM((basis, chan, chan), BF),
            pltpu.VMEM((members * own, basis * chan), BF),
            pltpu.VMEM((basis * own, depth), BF),
            pltpu.VMEM((basis * own, depth), BF),
            pltpu.VMEM((2, select.shape[0], chan), BF),
            pltpu.VMEM((2, 4, members * H, chan), BF),
            pltpu.VMEM(cells, BF),
            pltpu.VMEM(cells, BF),
            pltpu.VMEM((basis, chan, chan), BF),
            pltpu.SemaphoreType.DMA((6,)),
            pltpu.SemaphoreType.DMA((2, slots)),
            pltpu.SemaphoreType.DMA((2, slots)),
        ],
        compiler_params=pltpu.CompilerParams(
            collective_id=0, has_side_effects=True, vmem_limit_bytes=48 * 1024 * 1024
        ),
    )(
        members_in.reshape(cells), out_grad.reshape(cells), weight, table, cycle_block, half_width,
        jnp.asarray(pos), jnp.asarray(far, dtype=jnp.int32), jnp.asarray(select, dtype=BF),
        jnp.asarray(regroup, dtype=BF),
    )
    share = lax.psum_scatter(local_grad, "lon", scatter_dimension=1, tiled=True)
    weight_grad = lax.psum(share, ("ens", "lat")).astype(F32)
    return (res.reshape(members_in.shape), ing.reshape(members_in.shape), weight_grad)


def solution(mesh):
    cells = P("ens", "lat", "lon", None)
    return jax.shard_map(
        shards,
        mesh=mesh,
        in_specs=(cells, cells, P(), P(), P(), P()),
        out_specs=(cells, cells, P(None, "lon", None)),
        check_vma=False,
    )
```

time: 166 us -> 131 us (0.79)
  other arithmetic: 55.2 us -> 1.82 us
  Pallas kernels: 0 us -> 26.8 us
  waiting for transfers between devices: 56.9 us -> 82.4 us
  starting transfers between devices: 16.6 us -> 0.08 us
  matrix products: 10 us -> 0 us
  local copies, waits for them, and re-layouts: 12.5 us -> 5.47 us
    dynamic_update_slice x8 -> x0, other arithmetic: 47.4 us -> none  [spread_forward(): return lax.map(single, padded)]
    reduce_scatter x1, waiting for transfers between devices: 0.6 us -> 27.4 us  [shards(): share = lax.psum_scatter(local_grad, 'lon', scatter_dimension=1, tiled=True)]
    pallas_call x0 -> x1, Pallas kernels: none -> 26.8 us  [shards(): pl.pallas_call(functools.partial(block_kernel, dims), out_shape=[jax.Shap...]
    ppermute x8 -> x0, starting transfers between devices: 16.6 us -> none  [the longest x4 8.82 us: extended(): lax.ppermute(lax.slice_in_dim(block, block.shape[dim] - width, None, axis...]
    dot_general x4 -> x0, matrix products: 10 us -> none  [the longest x1 4.36 us: shards(): lax.dot_general(back.reshape(-1, K, C), weight, (((1, 2), (0, 2)), ((), (...]
    ppermute x8 -> x0, waiting for transfers between devices: 5.7 us -> none  [the longest x4 3.27 us: extended(): lax.ppermute(lax.slice_in_dim(block, 0, width, axis=dim), axis, backward)]
    another operation x2 -> x0, local copies, waits for them, and re-layouts: 4.84 us -> none
    psum x1, waiting for transfers between devices: 50.6 us -> 54.9 us  [shards(): weight_grad = lax.psum(share, ('ens', 'lat')).astype(F32)]
  transfers between devices with their start and end apart: 10 -> 2, of which waited for: 5 -> 2; matrix products, arithmetic and copies ran while one was open for 25% -> 0% of each run, Pallas kernels for 0% -> 0%
where the time goes in v1:
time: 131 us
  waiting for transfers between devices  82.4 us (63%)
  Pallas kernels  26.8 us (20%)
  between operations  14.2 us (11%)
  local copies, waits for them, and re-layouts  5.47 us (4%)
  other arithmetic  1.82 us (1%)
    psum x1, waiting for transfers between devices, shards(): weight_grad = lax.psum(share, ('ens', 'lat')).astype(F32)  54.9 us
    reduce_scatter x1, waiting for transfers between devices, shards(): share = lax.psum_scatter(local_grad, 'lon', scatter_dimension=1, tiled=True)  27.4 us
    pallas_call x1, Pallas kernels, shards(): pl.pallas_call(functools.partial(block_kernel, dims), out_shape=[jax.Shap...  26.8 us
    unnamed x19, local copies, waits for them, and re-layouts  4.19 us
  transfers between devices with their start and end apart: 2, of which 2 were waited for; matrix products, arithmetic and copies ran while one was open for 0% of the time, Pallas kernels for 0%

profile of v1, /device:TPU:0, one launch (start us, length us, event | category | flops | bytes accessed | tf_op | source)
XLA Modules:
  0.0 130.7 jit_solution(9585716378693436289)
XLA Ops:
  7.2 0.0 copy-start.5
  7.2 0.0 copy-start.1
  7.2 0.0 copy-start.4
  7.2 0.0 copy-start.6
  7.2 0.0 copy-start.7
  7.2 0.0 copy-start
  7.2 0.0 reduce-scatter.2.cloned.1.call-start
  7.3 0.9 copy.17.hw_ref
  8.1 0.9 copy.15
  9.1 0.1 reshape.23
  9.2 0.2 copy.16
  9.4 0.0 copy-done.5
  9.4 0.0 copy-done.1
  9.5 0.0 copy-done.4
  9.5 0.0 copy-done.6
  9.5 0.0 copy-done.7
  9.5 0.0 copy-done
  9.5 0.0 copy-start.2
  9.5 0.9 copy-done.2
  10.4 0.0 copy-start.3
  10.4 0.9 copy-done.3
  11.4 26.8 %shard_map.121 = (bf16[4,128,256]{2,1,0:T(8,128)(2,1)S(1)}, bf16[4,128,256]{2,1,0:T(8,128)(2,1)S(1)}, bf16[9,256,256]{2,1,0:T(8,128)(2,1)}) custom-call(bf16[4,128,256]{2,1,0:T(8,128)(2,1)S(1)} %bitcast.9, bf16[4,128,256]{2,1,0:T(8,128)(2,1)S(1)} %bitcast.10, bf16[9,256,256]{2,1,0:T(8,128)(2,1)S(1)} %copy-done, f32[8,96,128]{2,1,0:T(8,128)S(1)} %pad.4.basis_ref, ...), custom_call_target="tpu_custom_call" | custom-call | tf_op jit(solution)/shard_map/pallas_call | solution.py:340
  38.2 0.0 reduce-scatter.2.cloned.1.call-update
  38.2 0.0 all-reduce.3.cloned.1.call-start
  38.2 27.4 %reduce-scatter.2.cloned.1.call-done = bf16[9,64,256]{2,1,0:T(8,128)(2,1)} async-done(((bf16[9,256,256]{2,1,0:T(8,128)(2,1)}), bf16[9,64,256]{2,1,0:T(8,128)(2,1)}) %reduce-scatter.2.cloned.1.call-update) | async-done | bytes 294928 | tf_op jit(solution)/shard_map/reduce_scatter | solution.py:374
  65.6 0.0 all-reduce.3.cloned.1.call-update
  65.7 54.9 %all-reduce.3.cloned.1.call-done = bf16[9,64,256]{2,1,0:T(8,128)(2,1)} async-done(((bf16[9,64,256]{2,1,0:T(8,128)(2,1)}), bf16[9,64,256]{2,1,0:T(8,128)(2,1)}) %all-reduce.3.cloned.1.call-update) | async-done | bytes 294928 | tf_op jit(solution)/shard_map/psum | solution.py:375
  120.6 1.8 %convert_element_type.5 = f32[9,64,256]{2,1,0:T(8,128)} convert(bf16[9,64,256]{2,1,0:T(8,128)(2,1)} %all-reduce.3.cloned.1.call-done) | non-fusion elementwise | flops 147456 | bytes 884736 | tf_op jit(solution)/shard_map/convert_element_type | solution.py:375
  122.4 0.7 copy.21
  123.1 0.7 copy.22
  (1 shorter events, 0.0 us)
Async XLA Ops:
  7.2 2.3 %copy-start.5 = (bf16[64,64]{1,0:T(8,128)(2,1)S(1)}, bf16[64,64]{1,0:T(8,128)(2,1)}, u32[]{:S(2)}) copy-start(bf16[64,64]{1,0:T(8,128)(2,1)} %constant.14.clone.regroup_ref) | copy-start | bytes 24580
  7.2 2.3 %copy-start.1 = (bf16[320,512]{1,0:T(8,128)(2,1)S(1)}, bf16[320,512]{1,0:T(8,128)(2,1)}, u32[]{:S(2)}) copy-start(bf16[320,512]{1,0:T(8,128)(2,1)} %constant.13.clone.select_ref) | copy-start | bytes 983044
  7.2 2.3 %copy-start.4 = (s32[96,128]{1,0:T(8,128)S(1)}, s32[96,128]{1,0:T(8,128)}, u32[]{:S(2)}) copy-start(s32[96,128]{1,0:T(8,128)} %constant.12.clone.reach_ref) | copy-start | bytes 147460
  7.2 2.3 %copy-start.6 = (s32[8,256]{1,0:T(8,128)S(1)}, s32[8,256]{1,0:T(8,128)}, u32[]{:S(2)}) copy-start(s32[8,256]{1,0:T(8,128)} %constant.11.clone.pos_ref) | copy-start | bytes 24580
  7.2 2.3 %copy-start.7 = (s32[32]{0:T(128)S(1)}, s32[32]{0:T(128)}, u32[]{:S(2)}) copy-start(s32[32]{0:T(128)} %cb_ref.1) | copy-start | bytes 388
  7.2 2.3 %copy-start = (bf16[9,256,256]{2,1,0:T(8,128)(2,1)S(1)}, bf16[9,256,256]{2,1,0:T(8,128)(2,1)}, u32[]{:S(2)}) copy-start(bf16[9,256,256]{2,1,0:T(8,128)(2,1)} %w_hbm.1) | copy-start | bytes 3538948
  7.2 58.4 %reduce-scatter.2.cloned.1.call-start = ((), (), s32[]{:S(2)}) async-start(), calls=%async_computation.1 | async-start | bytes 1474560 | tf_op jit(solution)/shard_map/reduce_scatter | solution.py:374
  9.5 1.0 copy-start.2
  10.4 0.9 copy-start.3
  38.2 82.4 %all-reduce.3.cloned.1.call-start = ((), (), s32[]{:S(2)}) async-start(), calls=%async_computation.2 | async-start | bytes 589824 | tf_op jit(solution)/shard_map/psum | solution.py:375
Sparse Core Ops, SparseCore 0:
  38.3 27.2 reduce-scatter.1
  68.8 51.7 all-reduce.2

commit v2 on v1

--- a/solution.py
+++ b/solution.py
@@ -52,9 +52,10 @@
     dims,
     x_hbm, og_hbm, w_hbm, basis_ref, cb_ref, hw_ref, pos_ref, reach_ref, select_ref, regroup_ref,
     res_hbm, ing_hbm, wg_hbm,
-    xp, gp, og, w, feats, fwd, adj, packs, crecv, res, ing, wg, lsem, ssem, rsem,
+    xp, gp, og, w, feats, fwd, adj, packs, crecv, res, ing, wg, pair_in, plane_in, plane_sum,
+    lon_in, done, share, lsem, ssem, rsem, wssem, wrsem,
 ):
-    members, rows, cols, chan, basis, used, depth, lats, lons, total, scale = dims
+    members, rows, cols, chan, basis, used, depth, enss, lats, lons, total, scale = dims
     own = rows * cols
     rim = rows * H
     taps = 2 * H + 1
@@ -64,6 +65,14 @@
     east = lax.rem(lon + 1, lons)
     has_n = lat > 0
     has_s = lat < lats - 1
+    ens = lax.axis_index("ens")
+    chips = lats // 2
+    plane = enss * chips
+    core = lax.rem(lat, 2)
+    mine = ens * chips + lat // 2
+    held = chan // lons
+    piece = wg.shape[2] // plane
+    half = chan // 2
 
     load_x = pltpu.make_async_copy(x_hbm, xp.at[:, pl.ds(0, own), :], lsem.at[0])
     load_x.start()
@@ -79,6 +88,19 @@
 
     greet({"lon": west})
     greet({"lon": east})
+
+    def in_plane(step):
+        other = lax.rem(mine + step, plane)
+        return {"ens": other // chips, "lat": 2 * lax.rem(other, chips) + core}, other
+
+    def in_group(step):
+        other = lax.rem(ens * lats + lat + step, enss * lats)
+        return {"ens": other // lats, "lat": lax.rem(other, lats)}
+
+    for hop in range(1, enss * lats):
+        greet(in_group(hop))
+    for hop in range(1, lons):
+        greet({"lon": lax.rem(lon + hop, lons)})
 
     @pl.when(has_n)
     def _():
@@ -204,7 +226,8 @@
     clear(gp, crecv.at[1])
     load_x.wait()
     pl.semaphore_wait(
-        barrier, 2 + 3 * has_n.astype(jnp.int32) + 3 * has_s.astype(jnp.int32)
+        barrier,
+        lons + enss * lats + 3 * has_n.astype(jnp.int32) + 3 * has_s.astype(jnp.int32),
     )
     send(0)
 
@@ -288,12 +311,37 @@
             feats[:, k * chan : (k + 1) * chan], grad, (((0,), (0,)), ((), ())),
             preferred_element_type=F32,
         )
-        wg[k] = (part * scale).astype(BF)
-    save_wg = pltpu.make_async_copy(wg, wg_hbm, lsem.at[4])
-    save_wg.start()
-
+        part = (part * scale).astype(wg.dtype)
+        for z in range(lons):
+            for h in range(2):
+                wg[h, z, k * held : (k + 1) * held, :] = part[
+                    z * held : (z + 1) * held, h * half : (h + 1) * half
+                ]
+
+    def push(src, dst, slot, where):
+        one = pltpu.make_async_remote_copy(
+            src_ref=src, dst_ref=dst, send_sem=wssem.at[slot], recv_sem=wrsem.at[slot],
+            device_id=where, device_id_type=MESH,
+        )
+        one.start()
+        return one
+
+    pushed = [push(wg.at[1 - core], pair_in, 0, {"lat": lat + 1 - 2 * core})]
     receive(1)
     spread_all(adj, gp)
+
+    pushed[0].wait_recv()
+
+    def add_pair(z, carry):
+        wg[core, z] = (wg[core, z].astype(F32) + pair_in[z].astype(F32)).astype(BF)
+        return carry
+
+    lax.fori_loop(0, lons, add_pair, 0)
+    to_plane = []
+    for hop in range(1, plane):
+        where, other = in_plane(hop)
+        at = pl.ds(pl.multiple_of(other * piece, 16), piece)
+        to_plane.append(push(wg.at[core, :, at, :], plane_in.at[hop - 1], hop, where))
 
     def backward(m, carry):
         at = pl.ds(pl.multiple_of(m * own, own), own)
@@ -312,6 +360,45 @@
     sent(0)
     sent(1)
     save_res.wait()
+
+    for one in to_plane:
+        one.wait_recv()
+    own_piece = pl.ds(pl.multiple_of(mine * piece, 16), piece)
+
+    def add_plane(z, carry):
+        acc = wg[core, z, own_piece, :].astype(F32)
+        for hop in range(plane - 1):
+            acc = acc + plane_in[hop, z].astype(F32)
+        plane_sum[z] = acc.astype(BF)
+        return carry
+
+    lax.fori_loop(0, lons, add_plane, 0)
+    along = []
+    for hop in range(1, lons):
+        other = lax.rem(lon + hop, lons)
+        along.append(
+            push(plane_sum.at[other], lon_in.at[hop - 1], plane - 1 + hop, {"lon": other})
+        )
+    for one in along:
+        one.wait_recv()
+    acc = plane_sum[lon].astype(F32)
+    for hop in range(lons - 1):
+        acc = acc + lon_in[hop].astype(F32)
+    done[core, own_piece, :] = acc.astype(BF)
+    spot = done.at[core, own_piece, :]
+    around = [
+        push(spot, spot, plane + lons - 2 + hop, in_group(hop)) for hop in range(1, enss * lats)
+    ]
+    for one in around:
+        one.wait_recv()
+    for h in range(2):
+        full = done[h].astype(F32)
+        for k in range(basis):
+            share[k, :, h * half : (h + 1) * half] = full[k * held : (k + 1) * held]
+    save_wg = pltpu.make_async_copy(share, wg_hbm, lsem.at[4])
+    save_wg.start()
+    for one in pushed + to_plane + along + around:
+        one.wait_send()
     save_wg.wait()
     save_ing.wait()
 
@@ -320,15 +407,20 @@
     members, rows, cols, chan = members_in.shape
     blocks, basis, reach, taps = basis_blocks.shape
     own = rows * cols
-    lats, lons = lax.axis_size("lat"), lax.axis_size("lon")
+    enss, lats, lons = (lax.axis_size(axis) for axis in ("ens", "lat", "lon"))
+    plane = enss * lats // 2
+    held = chan // lons
+    span = -(-basis * held // (16 * plane)) * 16 * plane
+    piece = span // plane
+    half = chan // 2
     used, depth, pos, select, regroup = layout(members, rows, cols)
     lines = -(-basis * taps // 16) * 16
     table = jnp.transpose(basis_blocks, (0, 1, 3, 2)).reshape(blocks, basis * taps, reach)
     table = jnp.pad(table, ((0, 0), (0, lines - basis * taps), (0, 128 - reach)))
     far = np.broadcast_to(np.abs(np.arange(lines) % taps - H)[:, None], (lines, 128))
-    cell_count = members * lax.axis_size("ens") * own * lats * lons
+    cell_count = members * enss * own * lats * lons
     dims = (
-        members, rows, cols, chan, basis, used, depth, lats, lons, cycle_block.shape[0],
+        members, rows, cols, chan, basis, used, depth, enss, lats, lons, cycle_block.shape[0],
         1.0 / math.sqrt(cell_count),
     )
     anywhere = pl.BlockSpec(memory_space=pl.ANY)
@@ -337,12 +429,13 @@
     cells = (members, own, chan)
     padded = (members, depth, chan)
     slots = 6 + 2 * members
-    res, ing, local_grad = pl.pallas_call(
+    pushes = plane + lons - 1 + enss * lats - 1
+    res, ing, weight_grad = pl.pallas_call(
         functools.partial(block_kernel, dims),
         out_shape=[
             jax.ShapeDtypeStruct(cells, BF),
             jax.ShapeDtypeStruct(cells, BF),
-            jax.ShapeDtypeStruct((basis, chan, chan), BF),
+            jax.ShapeDtypeStruct((basis, held, chan), F32),
         ],
         in_specs=[anywhere] * 3 + [vmem, smem, smem] + [vmem] * 4,
         out_specs=[anywhere] * 3,
@@ -358,10 +451,18 @@
             pltpu.VMEM((2, 4, members * H, chan), BF),
             pltpu.VMEM(cells, BF),
             pltpu.VMEM(cells, BF),
-            pltpu.VMEM((basis, chan, chan), BF),
+            pltpu.VMEM((2, lons, span, half), BF),
+            pltpu.VMEM((lons, span, half), BF),
+            pltpu.VMEM((plane - 1, lons, piece, half), BF),
+            pltpu.VMEM((lons, piece, half), BF),
+            pltpu.VMEM((lons - 1, piece, half), BF),
+            pltpu.VMEM((2, span, half), BF),
+            pltpu.VMEM((basis, held, chan), F32),
             pltpu.SemaphoreType.DMA((6,)),
             pltpu.SemaphoreType.DMA((2, slots)),
             pltpu.SemaphoreType.DMA((2, slots)),
+            pltpu.SemaphoreType.DMA((pushes,)),
+            pltpu.SemaphoreType.DMA((pushes,)),
         ],
         compiler_params=pltpu.CompilerParams(
             collective_id=0, has_side_effects=True, vmem_limit_bytes=48 * 1024 * 1024
@@ -371,8 +472,6 @@
         jnp.asarray(pos), jnp.asarray(far, dtype=jnp.int32), jnp.asarray(select, dtype=BF),
         jnp.asarray(regroup, dtype=BF),
     )
-    share = lax.psum_scatter(local_grad, "lon", scatter_dimension=1, tiled=True)
-    weight_grad = lax.psum(share, ("ens", "lat")).astype(F32)
     return (res.reshape(members_in.shape), ing.reshape(members_in.shape), weight_grad)
 
 

time: 131 us -> 49.5 us (0.38)
  waiting for transfers between devices: 82.4 us -> 0 us
  Pallas kernels: 26.8 us -> 42.2 us
  between operations: 14.2 us -> 0.76 us
  other arithmetic: 1.82 us -> 0 us
    psum x1 -> x0, waiting for transfers between devices: 54.9 us -> none  [shards(): weight_grad = lax.psum(share, ('ens', 'lat')).astype(F32)]
    reduce_scatter x1 -> x0, waiting for transfers between devices: 27.4 us -> none  [shards(): share = lax.psum_scatter(local_grad, 'lon', scatter_dimension=1, tiled=True)]
    pallas_call x1, Pallas kernels: 26.8 us -> 42.2 us  [shards(): pl.pallas_call(functools.partial(block_kernel, dims), out_shape=[jax.Shap...]
    convert_element_type x1 -> x0, other arithmetic: 1.82 us -> none  [shards(): weight_grad = lax.psum(share, ('ens', 'lat')).astype(F32)]
    unnamed x19 -> x20, local copies, waits for them, and re-layouts: 4.19 us -> 5.02 us
  transfers between devices with their start and end apart: 2 -> 0, of which waited for: 2 -> 0; matrix products, arithmetic and copies ran while one was open for 0% -> 0% of each run, Pallas kernels for 0% -> 0%
where the time goes in v2:
time: 49.5 us; the launch traced here: 49.3 us
  Pallas kernels  42.2 us (85%)
  local copies, waits for them, and re-layouts  6.3 us (13%)
  between operations  0.76 us (2%)
    pallas_call x1, Pallas kernels, shards(): pl.pallas_call(functools.partial(block_kernel, dims), out_shape=[jax.Shap...  42.2 us
    unnamed x20, local copies, waits for them, and re-layouts  5.02 us

profile of v2, /device:TPU:0, one launch (start us, length us, event | category | flops | bytes accessed | tf_op | source)
XLA Modules:
  0.0 49.3 jit_solution(7818211545255949936)
XLA Ops:
  0.6 0.0 copy-start.5
  0.6 0.0 copy-start.1
  0.7 0.0 copy-start.4
  0.7 0.0 copy-start.6
  0.7 0.0 copy-start.7
  0.7 0.0 copy-start
  0.7 0.9 %copy.17.hw_ref = s32[32,3]{1,0:T(8,128)S(1)} copy(s32[32,3]{0,1:T(4,128)} %param.15) | data formatting | bytes 768 | tf_op args[5]
  1.6 0.9 %copy.15 = f32[8,9,9,3]{2,1,0,3:T(8,128)S(1)} copy(f32[8,9,9,3]{2,0,3,1:T(8,128)} %bitcast.11) | data formatting | bytes 15552 | tf_op jit(solution)/shard_map/transpose | solution.py:418
  2.5 0.1 reshape.23
  2.6 0.2 copy.16
  2.9 0.0 copy-done.5
  2.9 0.0 copy-done.1
  2.9 0.0 copy-done.4
  2.9 0.0 copy-done.6
  2.9 0.0 copy-done.7
  2.9 0.0 copy-done
  2.9 0.0 copy-start.2
  2.9 0.9 %copy-done.2 = bf16[4,8,16,256]{3,2,1,0:T(8,128)(2,1)S(1)} copy-done((bf16[4,8,16,256]{3,2,1,0:T(8,128)(2,1)S(1)}, bf16[4,8,16,256]{3,2,1,0:T(8,128)(2,1)}, u32[]{:S(2)}) %copy-start.2) | copy-done | bytes 262168
  3.9 0.0 copy-start.3
  3.9 0.9 %copy-done.3 = bf16[4,8,16,256]{3,2,1,0:T(8,128)(2,1)S(1)} copy-done((bf16[4,8,16,256]{3,2,1,0:T(8,128)(2,1)S(1)}, bf16[4,8,16,256]{3,2,1,0:T(8,128)(2,1)}, u32[]{:S(2)}) %copy-start.3) | copy-done | bytes 262168
  4.8 42.2 %shard_map.121 = (bf16[4,128,256]{2,1,0:T(8,128)(2,1)S(1)}, bf16[4,128,256]{2,1,0:T(8,128)(2,1)S(1)}, f32[9,64,256]{2,1,0:T(8,128)S(1)}) custom-call(bf16[4,128,256]{2,1,0:T(8,128)(2,1)S(1)} %bitcast.9, bf16[4,128,256]{2,1,0:T(8,128)(2,1)S(1)} %bitcast.10, bf16[9,256,256]{2,1,0:T(8,128)(2,1)S(1)} %copy-done, f32[8,96,128]{2,1,0:T(8,128)S(1)} %pad.4.basis_ref, ...), custom_call_target="tpu_custom_call" | custom-call | tf_op jit(solution)/shard_map/pallas_call | solution.py:433
  47.1 0.7 %copy.21 = bf16[4,8,16,256]{3,2,1,0:T(8,128)(2,1)} copy(bf16[4,8,16,256]{3,2,1,0:T(8,128)(2,1)S(1)} %bitcast.8) | data formatting | bytes 524288
  47.8 0.7 %copy.22 = bf16[4,8,16,256]{3,2,1,0:T(8,128)(2,1)} copy(bf16[4,8,16,256]{3,2,1,0:T(8,128)(2,1)S(1)} %bitcast.7) | data formatting | bytes 524288
  48.5 0.8 %copy.23 = f32[9,64,256]{2,1,0:T(8,128)} copy(f32[9,64,256]{2,1,0:T(8,128)S(1)} %get-tuple-element.14) | data formatting | bytes 1179648
  (1 shorter events, 0.0 us)
Async XLA Ops:
  0.6 2.2 %copy-start.5 = (bf16[64,64]{1,0:T(8,128)(2,1)S(1)}, bf16[64,64]{1,0:T(8,128)(2,1)}, u32[]{:S(2)}) copy-start(bf16[64,64]{1,0:T(8,128)(2,1)} %constant.14.clone.regroup_ref) | copy-start | bytes 24580
  0.6 2.2 %copy-start.1 = (bf16[320,512]{1,0:T(8,128)(2,1)S(1)}, bf16[320,512]{1,0:T(8,128)(2,1)}, u32[]{:S(2)}) copy-start(bf16[320,512]{1,0:T(8,128)(2,1)} %constant.13.clone.select_ref) | copy-start | bytes 983044
  0.7 2.2 %copy-start.4 = (s32[96,128]{1,0:T(8,128)S(1)}, s32[96,128]{1,0:T(8,128)}, u32[]{:S(2)}) copy-start(s32[96,128]{1,0:T(8,128)} %constant.12.clone.reach_ref) | copy-start | bytes 147460
  0.7 2.2 %copy-start.6 = (s32[8,256]{1,0:T(8,128)S(1)}, s32[8,256]{1,0:T(8,128)}, u32[]{:S(2)}) copy-start(s32[8,256]{1,0:T(8,128)} %constant.11.clone.pos_ref) | copy-start | bytes 24580
  0.7 2.2 %copy-start.7 = (s32[32]{0:T(128)S(1)}, s32[32]{0:T(128)}, u32[]{:S(2)}) copy-start(s32[32]{0:T(128)} %cb_ref.1) | copy-start | bytes 388
  0.7 2.2 %copy-start = (bf16[9,256,256]{2,1,0:T(8,128)(2,1)S(1)}, bf16[9,256,256]{2,1,0:T(8,128)(2,1)}, u32[]{:S(2)}) copy-start(bf16[9,256,256]{2,1,0:T(8,128)(2,1)} %w_hbm.1) | copy-start | bytes 3538948
  2.9 1.0 %copy-start.2 = (bf16[4,8,16,256]{3,2,1,0:T(8,128)(2,1)S(1)}, bf16[4,8,16,256]{3,2,1,0:T(8,128)(2,1)}, u32[]{:S(2)}) copy-start(bf16[4,8,16,256]{3,2,1,0:T(8,128)(2,1)} %param.10) | copy-start | bytes 786436
  3.9 0.9 %copy-start.3 = (bf16[4,8,16,256]{3,2,1,0:T(8,128)(2,1)S(1)}, bf16[4,8,16,256]{3,2,1,0:T(8,128)(2,1)}, u32[]{:S(2)}) copy-start(bf16[4,8,16,256]{3,2,1,0:T(8,128)(2,1)} %param.11) | copy-start | bytes 786436

commit v3 on v1

--- a/solution.py
+++ b/solution.py
@@ -29,15 +29,10 @@
     for p, (i, j) in enumerate(cells):
         pos[0, p], pos[1, p] = i, j
     own = rows * cols
-    index = lambda m, i, j: m * own + i * cols + j
-    picks = [index(m, i, j) for m in range(members) for i in range(rows) for j in range(H)]
-    picks += [
-        index(m, i, cols - H + j) for m in range(members) for i in range(rows) for j in range(H)
-    ]
-    for i in (0, rows - 1):
-        for first in (0, cols - H):
-            picks += [index(m, i, first + j) for m in range(members) for j in range(H)]
-    select = np.zeros((len(picks), members * own), np.float32)
+    picks = [i * cols + j for i in range(rows) for j in range(H)]
+    picks += [i * cols + cols - H + j for i in range(rows) for j in range(H)]
+    picks += [i * cols + f + j for i in (0, rows - 1) for f in (0, cols - H) for j in range(H)]
+    select = np.zeros((len(picks), own), np.float32)
     select[np.arange(len(picks)), picks] = 1
     corners = 4 * members * H
     regroup = np.zeros((corners, corners), np.float32)
@@ -50,11 +45,12 @@
 
 def block_kernel(
     dims,
-    x_hbm, og_hbm, w_hbm, basis_ref, cb_ref, hw_ref, pos_ref, reach_ref, select_ref, regroup_ref,
+    x_hbm, og_hbm, w_hbm, basis_ref, cb_ref, hw_ref, pos_ref, select_ref, regroup_ref,
     res_hbm, ing_hbm, wg_hbm,
-    xp, gp, og, w, feats, fwd, adj, packs, crecv, res, ing, wg, lsem, ssem, rsem,
+    xp, gp, og, w, feats, fwd, adj, packs, crecv, res, ing, wg, pair_in, plane_in, plane_sum,
+    lon_in, done, share, lines, lsem, ssem, rsem, wssem, wrsem,
 ):
-    members, rows, cols, chan, basis, used, depth, lats, lons, total, scale = dims
+    members, rows, cols, chan, basis, used, depth, enss, lats, lons, total, scale = dims
     own = rows * cols
     rim = rows * H
     taps = 2 * H + 1
@@ -64,6 +60,16 @@
     east = lax.rem(lon + 1, lons)
     has_n = lat > 0
     has_s = lat < lats - 1
+    ens = lax.axis_index("ens")
+    chips = lats // 2
+    plane = enss * chips
+    core = lax.rem(lat, 2)
+    mine = ens * chips + lat // 2
+    held = chan // lons
+    chunks, span = wg.shape[0], wg.shape[3]
+    piece = span // plane
+    group = 2 if members % 2 == 0 else 1
+    half = chan // 2
 
     load_x = pltpu.make_async_copy(x_hbm, xp.at[:, pl.ds(0, own), :], lsem.at[0])
     load_x.start()
@@ -79,6 +85,19 @@
 
     greet({"lon": west})
     greet({"lon": east})
+
+    def in_plane(step):
+        other = lax.rem(mine + step, plane)
+        return {"ens": other // chips, "lat": 2 * lax.rem(other, chips) + core}, other
+
+    def in_group(step):
+        other = lax.rem(ens * lats + lat + step, enss * lats)
+        return {"ens": other // lats, "lat": lax.rem(other, lats)}
+
+    for hop in range(1, enss * lats):
+        greet(in_group(hop))
+    for hop in range(1, lons):
+        greet({"lon": lax.rem(lon + hop, lons)})
 
     @pl.when(has_n)
     def _():
@@ -156,8 +175,18 @@
         c = copies(t)
         pad = (xp, gp)[t]
 
-        flat = pad[:, :own, :].reshape(members * own, chan)
-        packs[t] = jnp.dot(select_ref[...], flat, preferred_element_type=F32).astype(BF)
+        ends = []
+        for m in range(members):
+            got = jnp.dot(
+                select_ref[...], pad[m, :own, :], preferred_element_type=F32
+            )
+            packs[t, m * rim : (m + 1) * rim] = got[:rim].astype(BF)
+            packs[t, wide + m * rim : wide + (m + 1) * rim] = got[rim : 2 * rim].astype(BF)
+            ends.append(got[2 * rim :])
+        packs[t, 2 * wide :] = lax.dot_general(
+            regroup_ref[...], jnp.concatenate(ends, 0).astype(BF), (((0,), (0,)), ((), ())),
+            preferred_element_type=F32,
+        ).astype(BF)
         each(c, SIDES, lambda one: one.start())
 
         @pl.when(has_n)
@@ -204,49 +233,64 @@
     clear(gp, crecv.at[1])
     load_x.wait()
     pl.semaphore_wait(
-        barrier, 2 + 3 * has_n.astype(jnp.int32) + 3 * has_s.astype(jnp.int32)
+        barrier,
+        lons + enss * lats + 3 * has_n.astype(jnp.int32) + 3 * has_s.astype(jnp.int32),
     )
     send(0)
 
-    lane = lax.broadcasted_iota(jnp.int32, reach_ref.shape, 1)
+    blocks = basis_ref.shape[2]
+    sides = 2 * R + 1
+    tall = lines.shape[0] // basis
+    eye = (
+        lax.broadcasted_iota(jnp.int32, (tall, taps), 0)
+        == lax.broadcasted_iota(jnp.int32, (tall, taps), 1)
+    ).astype(F32).astype(BF)
+    for k in range(basis):
+        entries = basis_ref[k].reshape(sides * blocks, taps).astype(BF)
+        lines[k * tall : (k + 1) * tall, :] = lax.dot_general(
+            eye, entries, (((1,), (1,)), ((), ())), preferred_element_type=F32
+        )
+    lane = lax.broadcasted_iota(jnp.int32, lines.shape, 1)
+    far = jnp.abs(lax.broadcasted_iota(jnp.int32, lines.shape, 0) % tall - H)
     first = lat * rows
     cell_i, cell_j = pos_ref[0:1, :], pos_ref[1:2, :]
-    step = lax.broadcasted_iota(jnp.int32, (128, depth), 0)
+    entry = lax.broadcasted_iota(jnp.int32, (sides * blocks, depth), 0)
+    offset = entry // blocks
+    which = entry % blocks
     col = lax.broadcasted_iota(jnp.int32, (cols, depth), 0)
     ahead = cell_j - col + H
     behind = col - cell_j + H
 
-    def filters(i):
-        cyc = jnp.clip(first + i, 0, total - 1)
-        table = basis_ref[cb_ref[cyc]]
-        span = jnp.where(
-            lane == 0, hw_ref[cyc, 0], jnp.where(lane == 1, hw_ref[cyc, 1], hw_ref[cyc, 2])
+    def by_side(index, values):
+        return jnp.where(index == 0, values[0], jnp.where(index == 1, values[1], values[2]))
+
+    def expand(cycles, wanted, tap, dst, i):
+        cycles = [jnp.clip(first + cyc, 0, total - 1) for cyc in cycles]
+        span = by_side(lane // blocks, [hw_ref[r, cyc] for r, cyc in enumerate(cycles)])
+        table = jnp.where(far <= span, lines[...], 0.0).astype(BF)
+        block = by_side(offset, [cb_ref[cyc] for cyc in cycles])
+        hit = jnp.logical_and(wanted == offset, which == block)
+        spread = jnp.dot(
+            table, jnp.where(hit, 1.0, 0.0).astype(BF), preferred_element_type=F32
         )
-        return jnp.where(reach_ref[...] <= span, table, 0.0)
-
-    def expand(table, rowsel, offset, dst, i):
-        spread = jnp.dot(table.astype(BF), rowsel.astype(BF), preferred_element_type=F32)
         for k in range(basis):
             acc = jnp.zeros((cols, depth), F32)
             for d in range(taps):
-                line = spread[k * taps + d : k * taps + d + 1, :]
-                acc = jnp.where(offset == d, line, acc)
+                line = spread[k * tall + d : k * tall + d + 1, :]
+                acc = jnp.where(tap == d, line, acc)
             dst[pl.ds(pl.multiple_of(k * own + i * cols, cols), cols), :] = acc.astype(BF)
 
-    def build(i, carry):
-        here = filters(i)
-        onward = jnp.where(cell_i - i + R == step, 1.0, 0.0)
-        expand(here, onward, ahead, fwd, i)
-        table = jnp.where(
-            lane == 0, filters(i + 1), jnp.where(lane == 1, here, filters(i - 1))
-        )
-        back = jnp.where(i + R - cell_i == step, 1.0, 0.0)
-        expand(jnp.where(lane < 3, table, 0.0), back, behind, adj, i)
+    def build_forward(i, carry):
+        expand([i] * sides, cell_i - i + R, ahead, fwd, i)
         return carry
 
-    lax.fori_loop(0, rows, build, 0)
-
-    def spread_all(mat, pad):
+    def build_adjoint(i, carry):
+        expand([i + R - r for r in range(sides)], i + R - cell_i, behind, adj, i)
+        return carry
+
+    lax.fori_loop(0, rows, build_forward, 0)
+
+    def spread_some(mat, pad, begin, end):
         def one(m, carry):
             block = pad[m]
             at = pl.ds(pl.multiple_of(m * own, own), own)
@@ -256,95 +300,214 @@
                 ).astype(BF)
             return carry
 
-        lax.fori_loop(0, members, one, 0)
+        lax.fori_loop(begin, end, one, 0)
 
     receive(0)
-    spread_all(fwd, xp)
+    spread_some(fwd, xp, 0, members)
     load_w.wait()
     load_og.wait()
 
-    def forward(m, carry):
-        at = pl.ds(pl.multiple_of(m * own, own), own)
+    def forward(n, carry):
+        at = pl.ds(pl.multiple_of(n * (group * own), own), group * own)
         v = jnp.dot(
             feats[at, :], w[...].reshape(basis * chan, chan), preferred_element_type=F32
         )
         root = math.sqrt(2.0 / math.pi)
         vv = v * v
         th = jnp.tanh(root * (v + 0.044715 * (vv * v)))
-        half = 0.5 * (1.0 + th)
-        res[m] = (xp[m, :own, :].astype(F32) + v * half).astype(BF)
-        slope = half + 0.5 * v * (1.0 - th * th) * (root * (1.0 + 3 * 0.044715 * vv))
-        gp[m, :own, :] = (og[m].astype(F32) * slope).astype(BF)
+        half_up = 0.5 * (1.0 + th)
+        act = v * half_up
+        slope = half_up + 0.5 * v * (1.0 - th * th) * (root * (1.0 + 3 * 0.044715 * vv))
+        for g in range(group):
+            m = n * group + g
+            rows_g = slice(g * own, (g + 1) * own)
+            res[m] = (xp[m, :own, :].astype(F32) + act[rows_g]).astype(BF)
+            gp[m, :own, :] = (og[m].astype(F32) * slope[rows_g]).astype(BF)
         return carry
 
-    lax.fori_loop(0, members, forward, 0)
+    lax.fori_loop(0, members // group, forward, 0)
     send(1)
     save_res = pltpu.make_async_copy(res, res_hbm, lsem.at[3])
     save_res.start()
 
     grad = gp[:, :own, :].reshape(members * own, chan)
-    for k in range(basis):
-        part = lax.dot_general(
-            feats[:, k * chan : (k + 1) * chan], grad, (((0,), (0,)), ((), ())),
-            preferred_element_type=F32,
+    some = basis // chunks
+
+    def mix(n):
+        for u in range(some):
+            k = n * some + u
+            part = lax.dot_general(
+                feats[:, k * chan : (k + 1) * chan], grad, (((0,), (0,)), ((), ())),
+                preferred_element_type=F32,
+            )
+            part = (part * scale).astype(wg.dtype)
+            for z in range(lons):
+                for h in range(2):
+                    wg[n, h, z, u * held : (u + 1) * held, :] = part[
+                        z * held : (z + 1) * held, h * half : (h + 1) * half
+                    ]
+
+    def push(n, src, dst, slot, where):
+        one = pltpu.make_async_remote_copy(
+            src_ref=src, dst_ref=dst, send_sem=wssem.at[n, slot], recv_sem=wrsem.at[n, slot],
+            device_id=where, device_id_type=MESH,
         )
-        wg[k] = (part * scale).astype(BF)
-    save_wg = pltpu.make_async_copy(wg, wg_hbm, lsem.at[4])
-    save_wg.start()
-
-    receive(1)
-    spread_all(adj, gp)
-
-    def backward(m, carry):
-        at = pl.ds(pl.multiple_of(m * own, own), own)
-        acc = og[m].astype(F32)
+        one.start()
+        return one
+
+    own_piece = pl.ds(pl.multiple_of(mine * piece, 16), piece)
+    flight = {}
+
+    def to_pair(n):
+        flight[n, 0] = [
+            push(n, wg.at[n, 1 - core], pair_in.at[n], 0, {"lat": lat + 1 - 2 * core})
+        ]
+
+    def arrived(n, stage):
+        for one in flight[n, stage]:
+            one.wait_recv()
+
+    def to_plane(n):
+        arrived(n, 0)
+
+        def add(z, carry):
+            wg[n, core, z] = (wg[n, core, z].astype(F32) + pair_in[n, z].astype(F32)).astype(BF)
+            return carry
+
+        lax.fori_loop(0, lons, add, 0)
+        flight[n, 1] = []
+        for hop in range(1, plane):
+            where, other = in_plane(hop)
+            at = pl.ds(pl.multiple_of(other * piece, 16), piece)
+            flight[n, 1].append(
+                push(n, wg.at[n, core, :, at, :], plane_in.at[n, hop - 1], hop, where)
+            )
+
+    def to_lon(n):
+        arrived(n, 1)
+
+        def add(z, carry):
+            acc = wg[n, core, z, own_piece, :].astype(F32)
+            for hop in range(plane - 1):
+                acc = acc + plane_in[n, hop, z].astype(F32)
+            plane_sum[n, z] = acc.astype(BF)
+            return carry
+
+        lax.fori_loop(0, lons, add, 0)
+        flight[n, 2] = []
+        for hop in range(1, lons):
+            other = lax.rem(lon + hop, lons)
+            flight[n, 2].append(
+                push(
+                    n, plane_sum.at[n, other], lon_in.at[n, hop - 1], plane - 1 + hop,
+                    {"lon": other},
+                )
+            )
+
+    def to_group(n):
+        arrived(n, 2)
+        acc = plane_sum[n, lon].astype(F32)
+        for hop in range(lons - 1):
+            acc = acc + lon_in[n, hop].astype(F32)
+        done[n, core, own_piece, :] = acc.astype(BF)
+        spot = done.at[n, core, own_piece, :]
+        flight[n, 3] = [
+            push(n, spot, spot, plane + lons - 2 + hop, in_group(hop))
+            for hop in range(1, enss * lats)
+        ]
+
+    def keep(n):
+        arrived(n, 3)
+        for h in range(2):
+            full = done[n, h].astype(F32)
+            for u in range(some):
+                share[n * some + u, :, h * half : (h + 1) * half] = full[
+                    u * held : (u + 1) * held
+                ]
+
+    def backward(n, carry):
+        at = pl.ds(pl.multiple_of(n * (group * own), own), group * own)
+        acc = None
         for k in range(basis):
-            acc = acc + lax.dot_general(
+            term = lax.dot_general(
                 feats[at, k * chan : (k + 1) * chan], w[k], (((1,), (1,)), ((), ())),
                 preferred_element_type=F32,
             )
-        ing[m] = acc.astype(BF)
+            acc = term if acc is None else acc + term
+        for g in range(group):
+            m = n * group + g
+            ing[m] = (og[m].astype(F32) + acc[g * own : (g + 1) * own]).astype(BF)
         return carry
 
-    lax.fori_loop(0, members, backward, 0)
+    for n in range(chunks):
+        mix(n)
+        to_pair(n)
+        if n:
+            to_plane(n - 1)
+    lax.fori_loop(0, rows, build_adjoint, 0)
+    to_plane(chunks - 1)
+    receive(1)
+    spread_some(adj, gp, 0, members // 2)
+    to_lon(0)
+    spread_some(adj, gp, members // 2, members)
+    for n in range(1, chunks - 1):
+        to_lon(n)
+    lax.fori_loop(0, members // group, backward, 0)
     save_ing = pltpu.make_async_copy(ing, ing_hbm, lsem.at[5])
     save_ing.start()
+    to_group(0)
+    if chunks > 1:
+        to_lon(chunks - 1)
+    for n in range(1, chunks):
+        to_group(n)
     sent(0)
     sent(1)
     save_res.wait()
+    for n in range(chunks):
+        keep(n)
+    save_wg = pltpu.make_async_copy(share, wg_hbm, lsem.at[4])
+    save_wg.start()
+    for copies_sent in flight.values():
+        for one in copies_sent:
+            one.wait_send()
+    save_ing.wait()
     save_wg.wait()
-    save_ing.wait()
 
 
 def shards(members_in, out_grad, weight, basis_blocks, cycle_block, half_width):
     members, rows, cols, chan = members_in.shape
     blocks, basis, reach, taps = basis_blocks.shape
     own = rows * cols
-    lats, lons = lax.axis_size("lat"), lax.axis_size("lon")
+    enss, lats, lons = (lax.axis_size(axis) for axis in ("ens", "lat", "lon"))
+    plane = enss * lats // 2
+    held = chan // lons
+    chunks = 3 if basis % 3 == 0 else 1
+    span = -(-(basis // chunks) * held // (16 * plane)) * 16 * plane
+    piece = span // plane
+    half = chan // 2
     used, depth, pos, select, regroup = layout(members, rows, cols)
-    lines = -(-basis * taps // 16) * 16
-    table = jnp.transpose(basis_blocks, (0, 1, 3, 2)).reshape(blocks, basis * taps, reach)
-    table = jnp.pad(table, ((0, 0), (0, lines - basis * taps), (0, 128 - reach)))
-    far = np.broadcast_to(np.abs(np.arange(lines) % taps - H)[:, None], (lines, 128))
-    cell_count = members * lax.axis_size("ens") * own * lats * lons
+    tall = -(-taps // 16) * 16
+    cell_count = members * enss * own * lats * lons
     dims = (
-        members, rows, cols, chan, basis, used, depth, lats, lons, cycle_block.shape[0],
+        members, rows, cols, chan, basis, used, depth, enss, lats, lons, cycle_block.shape[0],
         1.0 / math.sqrt(cell_count),
     )
     anywhere = pl.BlockSpec(memory_space=pl.ANY)
+    hbm = pl.BlockSpec(memory_space=pltpu.HBM)
     vmem = pl.BlockSpec(memory_space=pltpu.VMEM)
     smem = pl.BlockSpec(memory_space=pltpu.SMEM)
     cells = (members, own, chan)
     padded = (members, depth, chan)
     slots = 6 + 2 * members
-    res, ing, local_grad = pl.pallas_call(
+    pushes = plane + lons - 1 + enss * lats - 1
+    res, ing, weight_grad = pl.pallas_call(
         functools.partial(block_kernel, dims),
         out_shape=[
             jax.ShapeDtypeStruct(cells, BF),
             jax.ShapeDtypeStruct(cells, BF),
-            jax.ShapeDtypeStruct((basis, chan, chan), BF),
+            jax.ShapeDtypeStruct((basis, held, chan), F32),
         ],
-        in_specs=[anywhere] * 3 + [vmem, smem, smem] + [vmem] * 4,
+        in_specs=[hbm] * 3 + [vmem, smem, smem] + [vmem] * 3,
         out_specs=[anywhere] * 3,
         scratch_shapes=[
             pltpu.VMEM(padded, BF),
@@ -354,25 +517,32 @@
             pltpu.VMEM((members * own, basis * chan), BF),
             pltpu.VMEM((basis * own, depth), BF),
             pltpu.VMEM((basis * own, depth), BF),
-            pltpu.VMEM((2, select.shape[0], chan), BF),
+            pltpu.VMEM((2, members * select.shape[0], chan), BF),
             pltpu.VMEM((2, 4, members * H, chan), BF),
             pltpu.VMEM(cells, BF),
             pltpu.VMEM(cells, BF),
-            pltpu.VMEM((basis, chan, chan), BF),
+            pltpu.VMEM((chunks, 2, lons, span, half), BF),
+            pltpu.VMEM((chunks, lons, span, half), BF),
+            pltpu.VMEM((chunks, plane - 1, lons, piece, half), BF),
+            pltpu.VMEM((chunks, lons, piece, half), BF),
+            pltpu.VMEM((chunks, lons - 1, piece, half), BF),
+            pltpu.VMEM((chunks, 2, span, half), BF),
+            pltpu.VMEM((basis, held, chan), F32),
+            pltpu.VMEM((basis * tall, reach * blocks), F32),
             pltpu.SemaphoreType.DMA((6,)),
             pltpu.SemaphoreType.DMA((2, slots)),
             pltpu.SemaphoreType.DMA((2, slots)),
+            pltpu.SemaphoreType.DMA((chunks, pushes)),
+            pltpu.SemaphoreType.DMA((chunks, pushes)),
         ],
         compiler_params=pltpu.CompilerParams(
             collective_id=0, has_side_effects=True, vmem_limit_bytes=48 * 1024 * 1024
         ),
     )(
-        members_in.reshape(cells), out_grad.reshape(cells), weight, table, cycle_block, half_width,
-        jnp.asarray(pos), jnp.asarray(far, dtype=jnp.int32), jnp.asarray(select, dtype=BF),
-        jnp.asarray(regroup, dtype=BF),
+        members_in.reshape(cells), out_grad.reshape(cells), weight,
+        jnp.transpose(basis_blocks, (1, 2, 0, 3)), cycle_block, half_width.T,
+        jnp.asarray(pos), jnp.asarray(select, dtype=BF), jnp.asarray(regroup, dtype=BF),
     )
-    share = lax.psum_scatter(local_grad, "lon", scatter_dimension=1, tiled=True)
-    weight_grad = lax.psum(share, ("ens", "lat")).astype(F32)
     return (res.reshape(members_in.shape), ing.reshape(members_in.shape), weight_grad)
 
 

time: 131 us -> 47.3 us (0.36)
  waiting for transfers between devices: 82.4 us -> 0 us
  between operations: 14.2 us -> 0.66 us
  Pallas kernels: 26.8 us -> 36.4 us
  local copies, waits for them, and re-layouts: 5.47 us -> 9.76 us
  other arithmetic: 1.82 us -> 0 us
    psum x1 -> x0, waiting for transfers between devices: 54.9 us -> none  [shards(): weight_grad = lax.psum(share, ('ens', 'lat')).astype(F32)]
    reduce_scatter x1 -> x0, waiting for transfers between devices: 27.4 us -> none  [shards(): share = lax.psum_scatter(local_grad, 'lon', scatter_dimension=1, tiled=True)]
    pallas_call x1, Pallas kernels: 26.8 us -> 36.4 us  [shards(): pl.pallas_call(functools.partial(block_kernel, dims), out_shape=[jax.Shap...]
    unnamed x19 -> x21, local copies, waits for them, and re-layouts: 4.19 us -> 9.76 us
    convert_element_type x1 -> x0, other arithmetic: 1.82 us -> none  [shards(): weight_grad = lax.psum(share, ('ens', 'lat')).astype(F32)]
  transfers between devices with their start and end apart: 2 -> 0, of which waited for: 2 -> 0; matrix products, arithmetic and copies ran while one was open for 0% -> 0% of each run, Pallas kernels for 0% -> 0%
where the time goes in v3:
time: 47.3 us; the launch traced here: 46.8 us
  Pallas kernels  36.4 us (77%)
  local copies, waits for them, and re-layouts  9.76 us (21%)
  between operations  0.66 us (1%)
    pallas_call x1, Pallas kernels, shards(): pl.pallas_call(functools.partial(block_kernel, dims), out_shape=[jax.Shap...  36.4 us
    unnamed x21, local copies, waits for them, and re-layouts  9.76 us

profile of v3, /device:TPU:0, one launch (start us, length us, event | category | flops | bytes accessed | tf_op | source)
XLA Modules:
  0.0 46.8 jit_solution(17146136482923129513)
XLA Ops:
  0.6 0.0 copy-start
  0.6 1.3 %copy-done = bf16[9,256,256]{2,1,0:T(8,128)(2,1)S(1)} copy-done((bf16[9,256,256]{2,1,0:T(8,128)(2,1)S(1)}, bf16[9,256,256]{2,1,0:T(8,128)(2,1)}, u32[]{:S(2)}) %copy-start) | copy-done | bytes 1179672
  1.9 0.0 copy-start.1
  1.9 0.9 %copy-done.1 = bf16[4,8,16,256]{3,2,1,0:T(8,128)(2,1)S(1)} copy-done((bf16[4,8,16,256]{3,2,1,0:T(8,128)(2,1)S(1)}, bf16[4,8,16,256]{3,2,1,0:T(8,128)(2,1)}, u32[]{:S(2)}) %copy-start.1) | copy-done | bytes 262168
  2.9 0.0 copy-start.2
  2.9 0.9 %copy-done.2 = bf16[4,8,16,256]{3,2,1,0:T(8,128)(2,1)S(1)} copy-done((bf16[4,8,16,256]{3,2,1,0:T(8,128)(2,1)S(1)}, bf16[4,8,16,256]{3,2,1,0:T(8,128)(2,1)}, u32[]{:S(2)}) %copy-start.2) | copy-done | bytes 262168
  3.8 0.0 copy-start.3
  3.8 0.9 %copy-done.3 = f32[8,9,3,9]{3,0,2,1:T(8,128)S(1)} copy-done((f32[8,9,3,9]{3,0,2,1:T(8,128)S(1)}, f32[8,9,3,9]{3,0,2,1:T(8,128)}, u32[]{:S(2)}) %copy-start.3) | copy-done | bytes 7800
  4.7 0.0 copy-start.4
  4.7 0.7 %copy-done.4 = bf16[80,128]{1,0:T(8,128)(2,1)S(1)} copy-done((bf16[80,128]{1,0:T(8,128)(2,1)S(1)}, bf16[80,128]{1,0:T(8,128)(2,1)}, u32[]{:S(2)}) %copy-start.4) | copy-done | bytes 20504
  5.4 0.0 copy-start.5
  5.4 0.7 %copy-done.5 = bf16[64,64]{1,0:T(8,128)(2,1)S(1)} copy-done((bf16[64,64]{1,0:T(8,128)(2,1)S(1)}, bf16[64,64]{1,0:T(8,128)(2,1)}, u32[]{:S(2)}) %copy-start.5) | copy-done | bytes 8216
  6.1 0.0 copy-start.6
  6.2 0.7 %copy-done.6 = s32[8,256]{1,0:T(8,128)S(1)} copy-done((s32[8,256]{1,0:T(8,128)S(1)}, s32[8,256]{1,0:T(8,128)}, u32[]{:S(2)}) %copy-start.6) | copy-done | bytes 8216
  6.8 0.0 copy-start.7
  6.8 0.7 %copy-done.7 = s32[32,3]{0,1:T(4,128)S(1)} copy-done((s32[32,3]{0,1:T(4,128)S(1)}, s32[32,3]{0,1:T(4,128)}, u32[]{:S(2)}) %copy-start.7) | copy-done | bytes 408
  7.5 0.0 copy-start.8
  7.5 0.7 %copy-done.8 = s32[32]{0:T(128)S(1)} copy-done((s32[32]{0:T(128)S(1)}, s32[32]{0:T(128)}, u32[]{:S(2)}) %copy-start.8) | copy-done | bytes 152
  8.2 36.4 %shard_map.112 = (bf16[4,128,256]{2,1,0:T(8,128)(2,1)S(1)}, bf16[4,128,256]{2,1,0:T(8,128)(2,1)S(1)}, f32[9,64,256]{2,1,0:T(8,128)S(1)}) custom-call(bf16[4,128,256]{2,1,0:T(8,128)(2,1)S(1)} %bitcast.6, bf16[4,128,256]{2,1,0:T(8,128)(2,1)S(1)} %bitcast.7, bf16[9,256,256]{2,1,0:T(8,128)(2,1)S(1)} %copy-done, f32[9,3,8,9]{3,2,1,0:T(8,128)S(1)} %bitcast.10, ...), custom_call_target="tpu_custom_call" | custom-call | tf_op jit(solution)/shard_map/pallas_call | solution.py:503
  44.6 0.7 %copy.15 = bf16[4,8,16,256]{3,2,1,0:T(8,128)(2,1)} copy(bf16[4,8,16,256]{3,2,1,0:T(8,128)(2,1)S(1)} %bitcast.9) | data formatting | bytes 524288
  45.3 0.7 %copy.16 = bf16[4,8,16,256]{3,2,1,0:T(8,128)(2,1)} copy(bf16[4,8,16,256]{3,2,1,0:T(8,128)(2,1)S(1)} %bitcast.8) | data formatting | bytes 524288
  46.0 0.8 %copy.17 = f32[9,64,256]{2,1,0:T(8,128)} copy(f32[9,64,256]{2,1,0:T(8,128)S(1)} %get-tuple-element.14) | data formatting | bytes 1179648
Async XLA Ops:
  0.6 1.3 %copy-start = (bf16[9,256,256]{2,1,0:T(8,128)(2,1)S(1)}, bf16[9,256,256]{2,1,0:T(8,128)(2,1)}, u32[]{:S(2)}) copy-start(bf16[9,256,256]{2,1,0:T(8,128)(2,1)} %w_hbm.1) | copy-start | bytes 3538948
  1.9 0.9 %copy-start.1 = (bf16[4,8,16,256]{3,2,1,0:T(8,128)(2,1)S(1)}, bf16[4,8,16,256]{3,2,1,0:T(8,128)(2,1)}, u32[]{:S(2)}) copy-start(bf16[4,8,16,256]{3,2,1,0:T(8,128)(2,1)} %param.9) | copy-start | bytes 786436
  2.9 0.9 %copy-start.2 = (bf16[4,8,16,256]{3,2,1,0:T(8,128)(2,1)S(1)}, bf16[4,8,16,256]{3,2,1,0:T(8,128)(2,1)}, u32[]{:S(2)}) copy-start(bf16[4,8,16,256]{3,2,1,0:T(8,128)(2,1)} %param.10) | copy-start | bytes 786436
  3.8 0.9 %copy-start.3 = (f32[8,9,3,9]{3,0,2,1:T(8,128)S(1)}, f32[8,9,3,9]{3,0,2,1:T(8,128)}, u32[]{:S(2)}) copy-start(f32[8,9,3,9]{3,0,2,1:T(8,128)} %param.12) | copy-start | bytes 23332
  4.7 0.7 %copy-start.4 = (bf16[80,128]{1,0:T(8,128)(2,1)S(1)}, bf16[80,128]{1,0:T(8,128)(2,1)}, u32[]{:S(2)}) copy-start(bf16[80,128]{1,0:T(8,128)(2,1)} %constant.7.clone.select_ref) | copy-start | bytes 61444
  5.4 0.7 %copy-start.5 = (bf16[64,64]{1,0:T(8,128)(2,1)S(1)}, bf16[64,64]{1,0:T(8,128)(2,1)}, u32[]{:S(2)}) copy-start(bf16[64,64]{1,0:T(8,128)(2,1)} %constant.8.clone.regroup_ref) | copy-start | bytes 24580
  6.1 0.7 %copy-start.6 = (s32[8,256]{1,0:T(8,128)S(1)}, s32[8,256]{1,0:T(8,128)}, u32[]{:S(2)}) copy-start(s32[8,256]{1,0:T(8,128)} %constant.6.clone.pos_ref) | copy-start | bytes 24580
  6.8 0.7 %copy-start.7 = (s32[32,3]{0,1:T(4,128)S(1)}, s32[32,3]{0,1:T(4,128)}, u32[]{:S(2)}) copy-start(s32[32,3]{0,1:T(4,128)} %param.14) | copy-start | bytes 1156
  7.5 0.7 %copy-start.8 = (s32[32]{0:T(128)S(1)}, s32[32]{0:T(128)}, u32[]{:S(2)}) copy-start(s32[32]{0:T(128)} %cb_ref.1) | copy-start | bytes 388

commit v4 on v3

--- a/solution.py
+++ b/solution.py
@@ -11,6 +11,7 @@
 
 R = 1
 H = 4
+VMEM = 63 * 1024 * 1024
 MESH = pl.DeviceIdType.MESH
 BF = jnp.bfloat16
 F32 = jnp.float32
@@ -45,10 +46,11 @@
 
 def block_kernel(
     dims,
-    x_hbm, og_hbm, w_hbm, basis_ref, cb_ref, hw_ref, pos_ref, select_ref, regroup_ref,
+    x_hbm, og_hbm, w_hbm, basis_hbm, cb_ref, hw_ref, pos_hbm, select_hbm, regroup_hbm,
     res_hbm, ing_hbm, wg_hbm,
     xp, gp, og, w, feats, fwd, adj, packs, crecv, res, ing, wg, pair_in, plane_in, plane_sum,
-    lon_in, done, share, lines, lsem, ssem, rsem, wssem, wrsem,
+    lon_in, done, share, lines,
+    basis_ref, pos_ref, select_ref, regroup_ref, lsem, ssem, rsem, wssem, wrsem,
 ):
     members, rows, cols, chan, basis, used, depth, enss, lats, lons, total, scale = dims
     own = rows * cols
@@ -73,6 +75,17 @@
 
     load_x = pltpu.make_async_copy(x_hbm, xp.at[:, pl.ds(0, own), :], lsem.at[0])
     load_x.start()
+    loads = [
+        pltpu.make_async_copy(src, dst, lsem.at[6 + n])
+        for n, (src, dst) in enumerate(
+            [
+                (select_hbm, select_ref), (regroup_hbm, regroup_ref),
+                (basis_hbm, basis_ref), (pos_hbm, pos_ref),
+            ]
+        )
+    ]
+    for one in loads:
+        one.start()
     load_og = pltpu.make_async_copy(og_hbm, og, lsem.at[1])
     load_og.start()
     load_w = pltpu.make_async_copy(w_hbm, w, lsem.at[2])
@@ -232,6 +245,8 @@
     clear(xp, crecv.at[0])
     clear(gp, crecv.at[1])
     load_x.wait()
+    for one in loads:
+        one.wait()
     pl.semaphore_wait(
         barrier,
         lons + enss * lats + 3 * has_n.astype(jnp.int32) + 3 * has_s.astype(jnp.int32),
@@ -494,7 +509,6 @@
     )
     anywhere = pl.BlockSpec(memory_space=pl.ANY)
     hbm = pl.BlockSpec(memory_space=pltpu.HBM)
-    vmem = pl.BlockSpec(memory_space=pltpu.VMEM)
     smem = pl.BlockSpec(memory_space=pltpu.SMEM)
     cells = (members, own, chan)
     padded = (members, depth, chan)
@@ -507,7 +521,7 @@
             jax.ShapeDtypeStruct(cells, BF),
             jax.ShapeDtypeStruct((basis, held, chan), F32),
         ],
-        in_specs=[hbm] * 3 + [vmem, smem, smem] + [vmem] * 3,
+        in_specs=[hbm] * 4 + [smem, smem] + [hbm] * 3,
         out_specs=[anywhere] * 3,
         scratch_shapes=[
             pltpu.VMEM(padded, BF),
@@ -529,14 +543,18 @@
             pltpu.VMEM((chunks, 2, span, half), BF),
             pltpu.VMEM((basis, held, chan), F32),
             pltpu.VMEM((basis * tall, reach * blocks), F32),
-            pltpu.SemaphoreType.DMA((6,)),
+            pltpu.VMEM((basis, reach, blocks, taps), F32),
+            pltpu.VMEM(pos.shape, jnp.int32),
+            pltpu.VMEM(select.shape, BF),
+            pltpu.VMEM(regroup.shape, BF),
+            pltpu.SemaphoreType.DMA((10,)),
             pltpu.SemaphoreType.DMA((2, slots)),
             pltpu.SemaphoreType.DMA((2, slots)),
             pltpu.SemaphoreType.DMA((chunks, pushes)),
             pltpu.SemaphoreType.DMA((chunks, pushes)),
         ],
         compiler_params=pltpu.CompilerParams(
-            collective_id=0, has_side_effects=True, vmem_limit_bytes=48 * 1024 * 1024
+            collective_id=0, has_side_effects=True, vmem_limit_bytes=VMEM
         ),
     )(
         members_in.reshape(cells), out_grad.reshape(cells), weight,

time: 47.3 us -> 42 us (0.89)
  local copies, waits for them, and re-layouts: 9.76 us -> 4.22 us
  Pallas kernels: 36.4 us -> 36.9 us
    unnamed x21 -> x5, local copies, waits for them, and re-layouts: 9.76 us -> 4.22 us
    pallas_call x1, Pallas kernels: 36.4 us -> 36.9 us  [shards(): pl.pallas_call(functools.partial(block_kernel, dims), out_shape=[jax.Shap...]
where the time goes in v4:
time: 42 us; the launch traced here: 41.8 us
  Pallas kernels  36.9 us (88%)
  local copies, waits for them, and re-layouts  4.22 us (10%)
  between operations  0.65 us (2%)
    pallas_call x1, Pallas kernels, shards(): pl.pallas_call(functools.partial(block_kernel, dims), out_shape=[jax.Shap...  36.9 us
    unnamed x5, local copies, waits for them, and re-layouts  4.22 us

profile of v4, /device:TPU:0, one launch (start us, length us, event | category | flops | bytes accessed | tf_op | source)
XLA Modules:
  0.0 41.8 jit_solution(3709805120718478406)
XLA Ops:
  0.6 36.9 %shard_map.112 = (bf16[4,128,256]{2,1,0:T(8,128)(2,1)}, bf16[4,128,256]{2,1,0:T(8,128)(2,1)}, f32[9,64,256]{2,1,0:T(8,128)}) custom-call(bf16[4,128,256]{2,1,0:T(8,128)(2,1)} %bitcast.6, bf16[4,128,256]{2,1,0:T(8,128)(2,1)} %bitcast.7, bf16[9,256,256]{2,1,0:T(8,128)(2,1)} %w_hbm.1, f32[9,3,8,9]{3,2,1,0:T(8,128)} %bitcast.10, s32[32]{0:T(128)} %cb_ref.1, ...), custom_call_target="tpu_custom_call" | custom-call | tf_op jit(solution)/shard_map/pallas_call | solution.py:517
  37.6 0.0 copy-start
  37.6 1.7 %copy.15 = bf16[4,8,16,256]{3,2,1,0:T(8,128)(2,1)} copy(bf16[4,8,16,256]{3,2,1,0:T(8,128)(2,1)} %bitcast.9) | data formatting | bytes 524288
  39.3 1.7 %copy.16 = bf16[4,8,16,256]{3,2,1,0:T(8,128)(2,1)} copy(bf16[4,8,16,256]{3,2,1,0:T(8,128)(2,1)} %bitcast.8) | data formatting | bytes 524288
  41.0 0.0 copy-done
  41.0 0.8 %copy.17 = f32[9,64,256]{2,1,0:T(8,128)} copy(f32[9,64,256]{2,1,0:T(8,128)S(1)} %copy-done) | data formatting | bytes 1179648
Async XLA Ops:
  37.6 3.4 %copy-start = (f32[9,64,256]{2,1,0:T(8,128)S(1)}, f32[9,64,256]{2,1,0:T(8,128)}, u32[]{:S(2)}) copy-start(f32[9,64,256]{2,1,0:T(8,128)} %get-tuple-element.14) | copy-start | bytes 1769476

commit v5 on v4

--- a/solution.py
+++ b/solution.py
@@ -347,15 +347,25 @@
 
     grad = gp[:, :own, :].reshape(members * own, chan)
     some = basis // chunks
+    unit = (
+        lax.broadcasted_iota(jnp.int32, (chan, chan), 0)
+        == lax.broadcasted_iota(jnp.int32, (chan, chan), 1)
+    ).astype(F32).astype(BF)
+
+    def turn(block):
+        return lax.dot_general(
+            unit, block, (((1,), (1,)), ((), ())), preferred_element_type=F32
+        ).astype(BF)
+
+    turned = turn(grad)
 
     def mix(n):
         for u in range(some):
             k = n * some + u
-            part = lax.dot_general(
-                feats[:, k * chan : (k + 1) * chan], grad, (((0,), (0,)), ((), ())),
-                preferred_element_type=F32,
+            part = jnp.dot(
+                turned, feats[:, k * chan : (k + 1) * chan], preferred_element_type=F32
             )
-            part = (part * scale).astype(wg.dtype)
+            part = turn((part * scale).astype(BF))
             for z in range(lons):
                 for h in range(2):
                     wg[n, h, z, u * held : (u + 1) * held, :] = part[
@@ -467,10 +477,12 @@
     spread_some(adj, gp, members // 2, members)
     for n in range(1, chunks - 1):
         to_lon(n)
-    lax.fori_loop(0, members // group, backward, 0)
+    turns = members // group
+    lax.fori_loop(0, turns // 2, backward, 0)
+    to_group(0)
+    lax.fori_loop(turns // 2, turns, backward, 0)
     save_ing = pltpu.make_async_copy(ing, ing_hbm, lsem.at[5])
     save_ing.start()
-    to_group(0)
     if chunks > 1:
         to_lon(chunks - 1)
     for n in range(1, chunks):
@@ -487,6 +499,19 @@
             one.wait_send()
     save_ing.wait()
     save_wg.wait()
+
+
+def place_kernel(res_in, ing_in, wg_in, res_out, ing_out, wg_out, sem):
+    moves = []
+    for src, dst in ((res_in, res_out), (ing_in, ing_out), (wg_in, wg_out)):
+        for part in range(src.shape[0]):
+            moves.append(
+                pltpu.make_async_copy(src.at[part], dst.at[part], sem.at[len(moves)])
+            )
+    for one in moves:
+        one.start()
+    for one in moves:
+        one.wait()
 
 
 def shards(members_in, out_grad, weight, basis_blocks, cycle_block, half_width):
@@ -561,6 +586,15 @@
         jnp.transpose(basis_blocks, (1, 2, 0, 3)), cycle_block, half_width.T,
         jnp.asarray(pos), jnp.asarray(select, dtype=BF), jnp.asarray(regroup, dtype=BF),
     )
+    held_back = [res, ing, weight_grad]
+    res, ing, weight_grad = pl.pallas_call(
+        place_kernel,
+        out_shape=[jax.ShapeDtypeStruct(a.shape, a.dtype) for a in held_back],
+        in_specs=[hbm] * 3,
+        out_specs=[hbm] * 3,
+        scratch_shapes=[pltpu.SemaphoreType.DMA((sum(a.shape[0] for a in held_back),))],
+        compiler_params=pltpu.CompilerParams(vmem_limit_bytes=VMEM),
+    )(*held_back)
     return (res.reshape(members_in.shape), ing.reshape(members_in.shape), weight_grad)
 
 

time: 42 us -> 73.4 us (1.75)
  Pallas kernels: 36.9 us -> 72.6 us
  local copies, waits for them, and re-layouts: 4.22 us -> 0 us
    pallas_call x0 -> x1, Pallas kernels: none -> 35 us  [shards(): pl.pallas_call(place_kernel, out_shape=[jax.ShapeDtypeStruct(a.shape, a.d...]
    unnamed x5 -> x0, local copies, waits for them, and re-layouts: 4.22 us -> none
where the time goes in v5:
time: 73.4 us; the launch traced here: 73.2 us
  Pallas kernels  72.6 us (99%)
    pallas_call x1, Pallas kernels, shards(): pl.pallas_call(functools.partial(block_kernel, dims), out_shape=[jax.Shap...  37.5 us
    pallas_call x1, Pallas kernels, shards(): pl.pallas_call(place_kernel, out_shape=[jax.ShapeDtypeStruct(a.shape, a.d...  35 us

profile of v5, /device:TPU:0, one launch (start us, length us, event | category | flops | bytes accessed | tf_op | source)
XLA Modules:
  0.0 73.2 jit_solution(15824198617919109227)
XLA Ops:
  0.6 37.5 %shard_map.112 = (bf16[4,128,256]{2,1,0:T(8,128)(2,1)}, bf16[4,128,256]{2,1,0:T(8,128)(2,1)}, f32[9,64,256]{2,1,0:T(8,128)}) custom-call(bf16[4,128,256]{2,1,0:T(8,128)(2,1)} %bitcast.6, bf16[4,128,256]{2,1,0:T(8,128)(2,1)} %bitcast.7, bf16[9,256,256]{2,1,0:T(8,128)(2,1)} %w_hbm.1, f32[9,3,8,9]{3,2,1,0:T(8,128)} %bitcast.8, s32[32]{0:T(128)} %cb_ref.1, ...), custom_call_target="tpu_custom_call" | custom-call | tf_op jit(solution)/shard_map/pallas_call | solution.py:542
  38.2 35.0 %shard_map.113 = (bf16[4,128,256]{2,1,0:T(8,128)(2,1)}, bf16[4,128,256]{2,1,0:T(8,128)(2,1)}, f32[9,64,256]{2,1,0:T(8,128)}) custom-call(bf16[4,128,256]{2,1,0:T(8,128)(2,1)} %get-tuple-element.9.res_in, bf16[4,128,256]{2,1,0:T(8,128)(2,1)} %get-tuple-element.10.ing_in, f32[9,64,256]{2,1,0:T(8,128)} %get-tuple-element.11.wg_in), custom_call_target="tpu_custom_call" | custom-call | tf_op jit(solution)/shard_map/pallas_call | solution.py:590

commit v6 on v5

--- a/solution.py
+++ b/solution.py
@@ -11,7 +11,7 @@
 
 R = 1
 H = 4
-VMEM = 63 * 1024 * 1024
+VMEM = 60 * 1024 * 1024
 MESH = pl.DeviceIdType.MESH
 BF = jnp.bfloat16
 F32 = jnp.float32
@@ -47,9 +47,9 @@
 def block_kernel(
     dims,
     x_hbm, og_hbm, w_hbm, basis_hbm, cb_ref, hw_ref, pos_hbm, select_hbm, regroup_hbm,
-    res_hbm, ing_hbm, wg_hbm,
-    xp, gp, og, w, feats, fwd, adj, packs, crecv, res, ing, wg, pair_in, plane_in, plane_sum,
-    lon_in, done, share, lines,
+    res, ing, share,
+    xp, gp, og, w, feats, fwd, adj, packs, crecv, wg, pair_in, plane_in, plane_sum,
+    lon_in, done, lines,
     basis_ref, pos_ref, select_ref, regroup_ref, lsem, ssem, rsem, wssem, wrsem,
 ):
     members, rows, cols, chan, basis, used, depth, enss, lats, lons, total, scale = dims
@@ -342,30 +342,17 @@
 
     lax.fori_loop(0, members // group, forward, 0)
     send(1)
-    save_res = pltpu.make_async_copy(res, res_hbm, lsem.at[3])
-    save_res.start()
 
     grad = gp[:, :own, :].reshape(members * own, chan)
     some = basis // chunks
-    unit = (
-        lax.broadcasted_iota(jnp.int32, (chan, chan), 0)
-        == lax.broadcasted_iota(jnp.int32, (chan, chan), 1)
-    ).astype(F32).astype(BF)
-
-    def turn(block):
-        return lax.dot_general(
-            unit, block, (((1,), (1,)), ((), ())), preferred_element_type=F32
-        ).astype(BF)
-
-    turned = turn(grad)
-
     def mix(n):
         for u in range(some):
             k = n * some + u
-            part = jnp.dot(
-                turned, feats[:, k * chan : (k + 1) * chan], preferred_element_type=F32
+            part = lax.dot_general(
+                feats[:, k * chan : (k + 1) * chan], grad, (((0,), (0,)), ((), ())),
+                preferred_element_type=F32,
             )
-            part = turn((part * scale).astype(BF))
+            part = (part * scale).astype(wg.dtype)
             for z in range(lons):
                 for h in range(2):
                     wg[n, h, z, u * held : (u + 1) * held, :] = part[
@@ -481,24 +468,17 @@
     lax.fori_loop(0, turns // 2, backward, 0)
     to_group(0)
     lax.fori_loop(turns // 2, turns, backward, 0)
-    save_ing = pltpu.make_async_copy(ing, ing_hbm, lsem.at[5])
-    save_ing.start()
     if chunks > 1:
         to_lon(chunks - 1)
     for n in range(1, chunks):
         to_group(n)
     sent(0)
     sent(1)
-    save_res.wait()
     for n in range(chunks):
         keep(n)
-    save_wg = pltpu.make_async_copy(share, wg_hbm, lsem.at[4])
-    save_wg.start()
     for copies_sent in flight.values():
         for one in copies_sent:
             one.wait_send()
-    save_ing.wait()
-    save_wg.wait()
 
 
 def place_kernel(res_in, ing_in, wg_in, res_out, ing_out, wg_out, sem):
@@ -532,7 +512,7 @@
         members, rows, cols, chan, basis, used, depth, enss, lats, lons, cycle_block.shape[0],
         1.0 / math.sqrt(cell_count),
     )
-    anywhere = pl.BlockSpec(memory_space=pl.ANY)
+    vmem = pl.BlockSpec(memory_space=pltpu.VMEM)
     hbm = pl.BlockSpec(memory_space=pltpu.HBM)
     smem = pl.BlockSpec(memory_space=pltpu.SMEM)
     cells = (members, own, chan)
@@ -542,12 +522,12 @@
     res, ing, weight_grad = pl.pallas_call(
         functools.partial(block_kernel, dims),
         out_shape=[
-            jax.ShapeDtypeStruct(cells, BF),
-            jax.ShapeDtypeStruct(cells, BF),
-            jax.ShapeDtypeStruct((basis, held, chan), F32),
+            pltpu.VMEM(cells, BF),
+            pltpu.VMEM(cells, BF),
+            pltpu.VMEM((basis, held, chan), F32),
         ],
         in_specs=[hbm] * 4 + [smem, smem] + [hbm] * 3,
-        out_specs=[anywhere] * 3,
+        out_specs=[vmem] * 3,
         scratch_shapes=[
             pltpu.VMEM(padded, BF),
             pltpu.VMEM(padded, BF),
@@ -558,15 +538,12 @@
             pltpu.VMEM((basis * own, depth), BF),
             pltpu.VMEM((2, members * select.shape[0], chan), BF),
             pltpu.VMEM((2, 4, members * H, chan), BF),
-            pltpu.VMEM(cells, BF),
-            pltpu.VMEM(cells, BF),
             pltpu.VMEM((chunks, 2, lons, span, half), BF),
             pltpu.VMEM((chunks, lons, span, half), BF),
             pltpu.VMEM((chunks, plane - 1, lons, piece, half), BF),
             pltpu.VMEM((chunks, lons, piece, half), BF),
             pltpu.VMEM((chunks, lons - 1, piece, half), BF),
             pltpu.VMEM((chunks, 2, span, half), BF),
-            pltpu.VMEM((basis, held, chan), F32),
             pltpu.VMEM((basis * tall, reach * blocks), F32),
             pltpu.VMEM((basis, reach, blocks, taps), F32),
             pltpu.VMEM(pos.shape, jnp.int32),
@@ -590,10 +567,10 @@
     res, ing, weight_grad = pl.pallas_call(
         place_kernel,
         out_shape=[jax.ShapeDtypeStruct(a.shape, a.dtype) for a in held_back],
-        in_specs=[hbm] * 3,
+        in_specs=[vmem] * 3,
         out_specs=[hbm] * 3,
         scratch_shapes=[pltpu.SemaphoreType.DMA((sum(a.shape[0] for a in held_back),))],
-        compiler_params=pltpu.CompilerParams(vmem_limit_bytes=VMEM),
+        compiler_params=pltpu.CompilerParams(vmem_limit_bytes=VMEM // 4),
     )(*held_back)
     return (res.reshape(members_in.shape), ing.reshape(members_in.shape), weight_grad)
 

time: 73.4 us -> 38.9 us (0.53)
  Pallas kernels: 72.6 us -> 38.1 us
    pallas_call x1, Pallas kernels: 35 us -> 1.12 us  [shards(): pl.pallas_call(place_kernel, out_shape=[jax.ShapeDtypeStruct(a.shape, a.d...]
where the time goes in v6:
time: 38.9 us; the launch traced here: 38.7 us
  Pallas kernels  38.1 us (98%)
  between operations  0.64 us (2%)
    pallas_call x1, Pallas kernels, shards(): pl.pallas_call(functools.partial(block_kernel, dims), out_shape=[pltpu.VM...  37 us
    pallas_call x1, Pallas kernels, shards(): pl.pallas_call(place_kernel, out_shape=[jax.ShapeDtypeStruct(a.shape, a.d...  1.12 us

profile of v6, /device:TPU:0, one launch (start us, length us, event | category | flops | bytes accessed | tf_op | source)
XLA Modules:
  0.0 38.7 jit_solution(10205337905226017090)
XLA Ops:
  0.6 37.0 %shard_map.112 = (bf16[4,128,256]{2,1,0:T(8,128)(2,1)S(1)}, bf16[4,128,256]{2,1,0:T(8,128)(2,1)S(1)}, f32[9,64,256]{2,1,0:T(8,128)S(1)}) custom-call(bf16[4,128,256]{2,1,0:T(8,128)(2,1)} %bitcast.6, bf16[4,128,256]{2,1,0:T(8,128)(2,1)} %bitcast.7, bf16[9,256,256]{2,1,0:T(8,128)(2,1)} %w_hbm.1, f32[9,3,8,9]{3,2,1,0:T(8,128)} %bitcast.8, s32[32]{0:T(128)} %cb_ref.1, ...), custom_call_target="tpu_custom_call" | custom-call | tf_op jit(solution)/shard_map/pallas_call | solution.py:522
  37.6 1.1 %shard_map.113 = (bf16[4,128,256]{2,1,0:T(8,128)(2,1)}, bf16[4,128,256]{2,1,0:T(8,128)(2,1)}, f32[9,64,256]{2,1,0:T(8,128)}) custom-call(bf16[4,128,256]{2,1,0:T(8,128)(2,1)S(1)} %get-tuple-element.9.res_in, bf16[4,128,256]{2,1,0:T(8,128)(2,1)S(1)} %get-tuple-element.10.ing_in, f32[9,64,256]{2,1,0:T(8,128)S(1)} %get-tuple-element.11.wg_in), custom_call_target="tpu_custom_call" | custom-call | tf_op jit(solution)/shard_map/pallas_call | solution.py:567

commit v7 on v6

--- a/solution.py
+++ b/solution.py
@@ -303,7 +303,7 @@
         expand([i + R - r for r in range(sides)], i + R - cell_i, behind, adj, i)
         return carry
 
-    lax.fori_loop(0, rows, build_forward, 0)
+    lax.fori_loop(0, rows, build_forward, 0, unroll=4 if rows % 4 == 0 else 1)
 
     def spread_some(mat, pad, begin, end):
         def one(m, carry):
@@ -315,7 +315,7 @@
                 ).astype(BF)
             return carry
 
-        lax.fori_loop(begin, end, one, 0)
+        lax.fori_loop(begin, end, one, 0, unroll=True)
 
     receive(0)
     spread_some(fwd, xp, 0, members)
@@ -340,7 +340,7 @@
             gp[m, :own, :] = (og[m].astype(F32) * slope[rows_g]).astype(BF)
         return carry
 
-    lax.fori_loop(0, members // group, forward, 0)
+    lax.fori_loop(0, members // group, forward, 0, unroll=True)
     send(1)
 
     grad = gp[:, :own, :].reshape(members * own, chan)
@@ -456,7 +456,7 @@
         to_pair(n)
         if n:
             to_plane(n - 1)
-    lax.fori_loop(0, rows, build_adjoint, 0)
+    lax.fori_loop(0, rows, build_adjoint, 0, unroll=4 if rows % 4 == 0 else 1)
     to_plane(chunks - 1)
     receive(1)
     spread_some(adj, gp, 0, members // 2)

time: 38.9 us -> 38 us (0.977)
  Pallas kernels: 38.1 us -> 37.2 us
    pallas_call x1, Pallas kernels: 37 us -> 36.1 us  [shards(): pl.pallas_call(functools.partial(block_kernel, dims), out_shape=[pltpu.VM...]
where the time goes in v7:
time: 38 us; the launch traced here: 37.9 us
  Pallas kernels  37.2 us (98%)
  between operations  0.64 us (2%)
    pallas_call x1, Pallas kernels, shards(): pl.pallas_call(functools.partial(block_kernel, dims), out_shape=[pltpu.VM...  36.1 us
    pallas_call x1, Pallas kernels, shards(): pl.pallas_call(place_kernel, out_shape=[jax.ShapeDtypeStruct(a.shape, a.d...  1.12 us

profile of v7, /device:TPU:0, one launch (start us, length us, event | category | flops | bytes accessed | tf_op | source)
XLA Modules:
  0.0 37.9 jit_solution(17217603713461904336)
XLA Ops:
  0.6 36.1 %shard_map.112 = (bf16[4,128,256]{2,1,0:T(8,128)(2,1)S(1)}, bf16[4,128,256]{2,1,0:T(8,128)(2,1)S(1)}, f32[9,64,256]{2,1,0:T(8,128)S(1)}) custom-call(bf16[4,128,256]{2,1,0:T(8,128)(2,1)} %bitcast.6, bf16[4,128,256]{2,1,0:T(8,128)(2,1)} %bitcast.7, bf16[9,256,256]{2,1,0:T(8,128)(2,1)} %w_hbm.1, f32[9,3,8,9]{3,2,1,0:T(8,128)} %bitcast.8, s32[32]{0:T(128)} %cb_ref.1, ...), custom_call_target="tpu_custom_call" | custom-call | tf_op jit(solution)/shard_map/pallas_call | solution.py:522
  36.7 1.1 %shard_map.113 = (bf16[4,128,256]{2,1,0:T(8,128)(2,1)}, bf16[4,128,256]{2,1,0:T(8,128)(2,1)}, f32[9,64,256]{2,1,0:T(8,128)}) custom-call(bf16[4,128,256]{2,1,0:T(8,128)(2,1)S(1)} %get-tuple-element.9.res_in, bf16[4,128,256]{2,1,0:T(8,128)(2,1)S(1)} %get-tuple-element.10.ing_in, f32[9,64,256]{2,1,0:T(8,128)S(1)} %get-tuple-element.11.wg_in), custom_call_target="tpu_custom_call" | custom-call | tf_op jit(solution)/shard_map/pallas_call | solution.py:567

commit v8 on v7

--- a/solution.py
+++ b/solution.py
@@ -49,7 +49,7 @@
     x_hbm, og_hbm, w_hbm, basis_hbm, cb_ref, hw_ref, pos_hbm, select_hbm, regroup_hbm,
     res, ing, share,
     xp, gp, og, w, feats, fwd, adj, packs, crecv, wg, pair_in, plane_in, plane_sum,
-    lon_in, done, lines,
+    lon_in, done, lon_wide, wide_sum, lines,
     basis_ref, pos_ref, select_ref, regroup_ref, lsem, ssem, rsem, wssem, wrsem,
 ):
     members, rows, cols, chan, basis, used, depth, enss, lats, lons, total, scale = dims
@@ -379,7 +379,7 @@
         for one in flight[n, stage]:
             one.wait_recv()
 
-    def to_plane(n):
+    def add_pair(n):
         arrived(n, 0)
 
         def add(z, carry):
@@ -387,6 +387,35 @@
             return carry
 
         lax.fori_loop(0, lons, add, 0)
+
+    def lon_before_plane(n):
+        add_pair(n)
+        flight[n, 2] = []
+        for hop in range(1, lons):
+            other = lax.rem(lon + hop, lons)
+            flight[n, 2].append(
+                push(
+                    n, wg.at[n, core, other], lon_wide.at[hop - 1], plane - 1 + hop,
+                    {"lon": other},
+                )
+            )
+
+    def plane_after_lon(n):
+        arrived(n, 2)
+        acc = wg[n, core, lon].astype(F32)
+        for hop in range(lons - 1):
+            acc = acc + lon_wide[hop].astype(F32)
+        wide_sum[...] = acc.astype(BF)
+        flight[n, 1] = []
+        for hop in range(1, plane):
+            where, other = in_plane(hop)
+            at = pl.ds(pl.multiple_of(other * piece, 16), piece)
+            flight[n, 1].append(
+                push(n, wide_sum.at[at, :], plane_in.at[n, hop - 1, 0], hop, where)
+            )
+
+    def to_plane(n):
+        add_pair(n)
         flight[n, 1] = []
         for hop in range(1, plane):
             where, other = in_plane(hop)
@@ -417,10 +446,16 @@
             )
 
     def to_group(n):
-        arrived(n, 2)
-        acc = plane_sum[n, lon].astype(F32)
-        for hop in range(lons - 1):
-            acc = acc + lon_in[n, hop].astype(F32)
+        if n == 0:
+            arrived(n, 1)
+            acc = wide_sum[own_piece, :].astype(F32)
+            for hop in range(plane - 1):
+                acc = acc + plane_in[n, hop, 0].astype(F32)
+        else:
+            arrived(n, 2)
+            acc = plane_sum[n, lon].astype(F32)
+            for hop in range(lons - 1):
+                acc = acc + lon_in[n, hop].astype(F32)
         done[n, core, own_piece, :] = acc.astype(BF)
         spot = done.at[n, core, own_piece, :]
         flight[n, 3] = [
@@ -454,13 +489,18 @@
     for n in range(chunks):
         mix(n)
         to_pair(n)
-        if n:
+        if n == 1:
+            lon_before_plane(0)
+        if n > 1:
             to_plane(n - 1)
     lax.fori_loop(0, rows, build_adjoint, 0, unroll=4 if rows % 4 == 0 else 1)
-    to_plane(chunks - 1)
+    if chunks > 1:
+        to_plane(chunks - 1)
+    else:
+        lon_before_plane(0)
     receive(1)
     spread_some(adj, gp, 0, members // 2)
-    to_lon(0)
+    plane_after_lon(0)
     spread_some(adj, gp, members // 2, members)
     for n in range(1, chunks - 1):
         to_lon(n)
@@ -544,6 +584,8 @@
             pltpu.VMEM((chunks, lons, piece, half), BF),
             pltpu.VMEM((chunks, lons - 1, piece, half), BF),
             pltpu.VMEM((chunks, 2, span, half), BF),
+            pltpu.VMEM((lons - 1, span, half), BF),
+            pltpu.VMEM((span, half), BF),
             pltpu.VMEM((basis * tall, reach * blocks), F32),
             pltpu.VMEM((basis, reach, blocks, taps), F32),
             pltpu.VMEM(pos.shape, jnp.int32),

time: 38 us -> 39 us (1.026)
  Pallas kernels: 37.2 us -> 38.1 us
    pallas_call x1, Pallas kernels: 36.1 us -> 37 us  [shards(): pl.pallas_call(functools.partial(block_kernel, dims), out_shape=[pltpu.VM...]
where the time goes in v8:
time: 39 us; the launch traced here: 38.8 us
  Pallas kernels  38.1 us (98%)
  between operations  0.64 us (2%)
    pallas_call x1, Pallas kernels, shards(): pl.pallas_call(functools.partial(block_kernel, dims), out_shape=[pltpu.VM...  37 us
    pallas_call x1, Pallas kernels, shards(): pl.pallas_call(place_kernel, out_shape=[jax.ShapeDtypeStruct(a.shape, a.d...  1.12 us

profile of v8, /device:TPU:0, one launch (start us, length us, event | category | flops | bytes accessed | tf_op | source)
XLA Modules:
  0.0 38.8 jit_solution(17037947309280437620)
XLA Ops:
  0.6 37.0 %shard_map.112 = (bf16[4,128,256]{2,1,0:T(8,128)(2,1)S(1)}, bf16[4,128,256]{2,1,0:T(8,128)(2,1)S(1)}, f32[9,64,256]{2,1,0:T(8,128)S(1)}) custom-call(bf16[4,128,256]{2,1,0:T(8,128)(2,1)} %bitcast.6, bf16[4,128,256]{2,1,0:T(8,128)(2,1)} %bitcast.7, bf16[9,256,256]{2,1,0:T(8,128)(2,1)} %w_hbm.1, f32[9,3,8,9]{3,2,1,0:T(8,128)} %bitcast.8, s32[32]{0:T(128)} %cb_ref.1, ...), custom_call_target="tpu_custom_call" | custom-call | tf_op jit(solution)/shard_map/pallas_call | solution.py:562
  37.7 1.1 %shard_map.113 = (bf16[4,128,256]{2,1,0:T(8,128)(2,1)}, bf16[4,128,256]{2,1,0:T(8,128)(2,1)}, f32[9,64,256]{2,1,0:T(8,128)}) custom-call(bf16[4,128,256]{2,1,0:T(8,128)(2,1)S(1)} %get-tuple-element.9.res_in, bf16[4,128,256]{2,1,0:T(8,128)(2,1)S(1)} %get-tuple-element.10.ing_in, f32[9,64,256]{2,1,0:T(8,128)S(1)} %get-tuple-element.11.wg_in), custom_call_target="tpu_custom_call" | custom-call | tf_op jit(solution)/shard_map/pallas_call | solution.py:609
